TPU v7x, 32 devices: a whole 2x2x4 slice. The times are simulated.
32 devices in a mesh: dp: 8 (over z, x), tensor: 4 (over y, core).
Axes of the slice: x: 2, y: 2, z: 4, core: 2. Of those that a mesh axis runs over, the one named last changes fastest.
Arguments:
- tokens: bfloat16 [16, 1024, 768], P('dp'), may hold values from -6 to 6
- cotangent: bfloat16 [16, 1024, 768], P('dp'), may hold values from -6 to 6
- lengths: int32 [16], replicated, may hold values from 64 to 1024, as said below
- perm: int32 [16], replicated, may hold values from 0 to 15, as said below
- norm_gain: float32 [768], replicated, may hold values from 0.5 to 1.5
- proj_gate: bfloat16 [768, 1536], P(None, 'tensor'), may hold values from -0.21875 to 0.21875
- proj_inner: bfloat16 [768, 1536], P(None, 'tensor'), may hold values from -0.21875 to 0.21875
- state_input_matrix: bfloat16 [768, 256], replicated, may hold values from -0.21875 to 0.21875
- stepsize_matrix: bfloat16 [768, 24], P(None, 'tensor'), may hold values from -0.21875 to 0.21875
- conv_weight: float32 [4, 1536], P(None, 'tensor'), may hold values from -3 to 3
- conv_offset: float32 [1536], P('tensor'), may hold values from -3 to 3
- conv_bc_weight: float32 [4, 256], replicated, may hold values from -3 to 3
- conv_bc_offset: float32 [256], replicated, may hold values from -3 to 3
- step_offset: float32 [24], P('tensor'), may hold values from -5 to -1
- decay_log: float32 [24], P('tensor'), may hold values from 0 to 2.7
- skip_gain: float32 [24], P('tensor'), may hold values from 0.5 to 1.5
- out_gain: float32 [1536], P('tensor'), may hold values from 0.5 to 1.5
- output_matrix: bfloat16 [1536, 768], P('tensor'), may hold values from -0.15625 to 0.15625
Outputs:
- block_out: bfloat16 [16, 1024, 768], P('dp')
- tokens_grad: bfloat16 [16, 1024, 768], P('dp')
- grad_norm_gain: float32 [768], replicated
- grad_proj_gate: float32 [768, 1536], P('dp', 'tensor')
- grad_proj_inner: float32 [768, 1536], P('dp', 'tensor')
- grad_proj_bc: float32 [768, 256], P('dp')
- grad_proj_step: float32 [768, 24], P('dp', 'tensor')
- grad_conv_weight: float32 [4, 1536], P(None, 'tensor')
- grad_conv_offset: float32 [1536], P('tensor')
- grad_conv_bc_weight: float32 [4, 256], replicated
- grad_conv_bc_offset: float32 [256], replicated
- grad_step_offset: float32 [24], P('tensor')
- grad_decay_log: float32 [24], P('tensor')
- grad_skip_gain: float32 [24], P('tensor')
- grad_out_gain: float32 [1536], P('tensor')
- grad_proj_out: float32 [1536, 768], P('tensor', 'dp')
Inputs may be any that keep to these rules, and one draw needn't show every extreme that they name: `lengths`: positions at or past a sequence's length are padding. Some sequence has exactly 1024 live tokens in every draw. Slot 2i holds sequence 2i; slot 2i+1 holds sequence 2i+1 or the sequence 2j+1, where j is the index of dp that differs from i in its highest bit; perm is its own inverse.
All inputs are finite; a program needn't handle non-finite values.
Results may differ from a plain program's by a relative error of at most 0.0086.
Values may be sent and summed in bfloat16 or wider, within the bound.
No kernel may reach another device: no remote copies, remote signals or barrier semaphores. Data moves between devices by JAX's collectives and lax.ppermute only.
A program may use at most 128 MiB of HBM per device.

v0:
```python
import jax
import jax.numpy as jnp
from jax import lax
from jax.sharding import PartitionSpec as P

GROUP = 256


EPS = 1e-05
HIGH = lax.Precision.HIGHEST


def partner_2(value, axis, stride):
    mask = 2**stride
    pairs = [(source, source ^ mask) for source in range(lax.axis_size(axis))]
    return lax.ppermute(value, axis, pairs)


def causal_conv(before, weight, offset):
    width = weight.shape[0]
    length = before.shape[1]
    padded = jnp.pad(before, ((0, 0), (width - 1, 0), (0, 0)))
    summed = offset + weight[0] * padded[:, 0:length]
    for tap in range(1, width):
        summed = summed + weight[tap] * padded[:, tap : tap + length]
    return jax.nn.silu(summed)


def bc_conv(state_input_before, weight, offset):
    both = causal_conv(state_input_before, weight, offset)
    middle = both.shape[-1] // 2
    return (both[..., :middle], both[..., middle:])


def state_pass(entering, inputs):
    decay, fresh = inputs
    return (entering * decay[..., None, None] + fresh, entering)


def block_scan(values, bmat, cmat, steps, rate):
    slots, length, heads, hsize = values.shape
    state = bmat.shape[-1]
    blocks = length // GROUP
    vblock = values.reshape(slots, blocks, GROUP, heads, hsize)
    bblock = bmat.reshape(slots, blocks, GROUP, state)
    cblock = cmat.reshape(slots, blocks, GROUP, state)
    sblock = jnp.moveaxis(steps.reshape(slots, blocks, GROUP, heads), 3, 2)
    cumul = jnp.cumsum(sblock * rate[:, None], axis=3)
    places = jnp.arange(GROUP)
    causal = places[:, None] >= places[None, :]
    spread = cumul[..., :, None] - cumul[..., None, :]
    weights = jnp.exp(jnp.where(causal, spread, -1e30))
    scores = jnp.einsum("sbqn,sbkn->sbqk", cblock, bblock, precision=HIGH)
    mixing = weights * scores[:, :, None] * sblock[:, :, :, None, :]
    inside = jnp.einsum("sbhqk,sbkhp->sbqhp", mixing, vblock, precision=HIGH)
    ending = cumul[..., -1:]
    to_end = jnp.exp(ending - cumul) * sblock
    fresh = jnp.einsum("sbhk,sbkn,sbkhp->sbhnp", to_end, bblock, vblock, precision=HIGH)
    anchor = jnp.zeros((slots, heads, state, hsize), jnp.float32)
    leftover, entering = lax.scan(
        state_pass, anchor, (jnp.moveaxis(jnp.exp(ending[..., 0]), 1, 0), jnp.moveaxis(fresh, 1, 0))
    )
    entering = jnp.moveaxis(entering, 0, 1)
    outside = jnp.einsum("sbqn,sbhnp->sbqhp", cblock, entering, precision=HIGH)
    outside = outside * jnp.moveaxis(jnp.exp(cumul), 2, 3)[..., None]
    return (inside + outside).reshape(slots, length, heads, hsize)


def mixer(
    inner_pre,
    bmat,
    cmat,
    stepsize_before,
    gate_pre,
    conv_weight,
    conv_offset,
    step_offset,
    decay_log,
    skip_gain,
):
    active = causal_conv(inner_pre, conv_weight, conv_offset)
    slots, length, width = active.shape
    heads = step_offset.shape[0]
    values = active.reshape(slots, length, heads, width // heads)
    steps = jax.nn.softplus(stepsize_before + step_offset)
    scanned = (
        block_scan(values, bmat, cmat, steps, -jnp.exp(decay_log)) + skip_gain[:, None] * values
    )
    return scanned.reshape(slots, length, width) * jax.nn.silu(gate_pre)


def body(
    tokens,
    cotangent,
    lengths,
    perm,
    norm_gain,
    proj_gate,
    proj_inner,
    state_input_matrix,
    stepsize_matrix,
    conv_weight,
    conv_offset,
    conv_bc_weight,
    conv_bc_offset,
    step_offset,
    decay_log,
    skip_gain,
    out_gain,
    output_matrix,
):
    slots, length, width = tokens.shape
    inner_dev = proj_gate.shape[1]
    inner_all = inner_dev * lax.axis_size("tensor")
    top_bit = lax.axis_size("dp").bit_length() - 2
    first_slot = lax.axis_index("dp") * slots
    own_order = lax.dynamic_slice_in_dim(perm, first_slot, slots)
    moved = own_order != first_slot + jnp.arange(slots, dtype=jnp.int32)
    partner = partner_2(tokens[1:], "dp", top_bit)
    dealt = jnp.concatenate([tokens[:1], jnp.where(moved[1], partner, tokens[1:])], axis=0)
    live_len = lengths[own_order]
    live_mask = (jnp.arange(length)[None, :] < live_len[:, None]).astype(jnp.float32)
    dealt_float = dealt.astype(jnp.float32)
    inv_rms = lax.rsqrt(jnp.mean(dealt_float * dealt_float, axis=-1, keepdims=True) + EPS)
    normal_hat = dealt_float * inv_rms
    normalized_rows = (normal_hat * norm_gain).astype(jnp.bfloat16)
    joint_matrix = jnp.concatenate([proj_gate, proj_inner], axis=1)
    joint_before = jnp.einsum(
        "qxm,mp->qxp", normalized_rows, joint_matrix, preferred_element_type=jnp.float32
    )
    gate_pre = joint_before[..., :inner_dev]
    inner_pre = joint_before[..., inner_dev:]
    stepsize_before = jnp.einsum(
        "qxm,mp->qxp", normalized_rows, stepsize_matrix, preferred_element_type=jnp.float32
    )
    state_input_before = jnp.einsum(
        "qxm,mp->qxp", normalized_rows, state_input_matrix, preferred_element_type=jnp.float32
    )
    (bmat, cmat), bc_back = jax.vjp(bc_conv, state_input_before, conv_bc_weight, conv_bc_offset)
    gated, mix_back = jax.vjp(
        mixer,
        inner_pre,
        bmat,
        cmat,
        stepsize_before,
        gate_pre,
        conv_weight,
        conv_offset,
        step_offset,
        decay_log,
        skip_gain,
    )
    squares = lax.psum(jnp.sum(gated * gated, axis=-1), "tensor")
    rgate = lax.rsqrt(squares / inner_all + EPS)[..., None]
    gated_rms_output = (gated * rgate * out_gain).astype(jnp.bfloat16)
    partial_out = jnp.einsum(
        "wth,hu->wtu", gated_rms_output, output_matrix, preferred_element_type=jnp.float32
    )
    branch = lax.psum(partial_out, "tensor")
    block_out = (dealt_float + live_mask[..., None] * branch).astype(jnp.bfloat16)
    cot_float = cotangent.astype(jnp.float32)
    mixer_branch_gradient = cotangent * live_mask[..., None].astype(jnp.bfloat16)
    grad_proj_out = jnp.einsum(
        "tvw,tvp->wp", gated_rms_output, mixer_branch_gradient, preferred_element_type=jnp.float32
    )
    norm_out_grad = jnp.einsum(
        "mwx,cx->mwc", mixer_branch_gradient, output_matrix, preferred_element_type=jnp.float32
    )
    grad_out_gain = jnp.sum(norm_out_grad * gated * rgate, axis=(0, 1))
    scaled = norm_out_grad * out_gain
    cross = lax.psum(jnp.sum(scaled * gated, axis=-1), "tensor")
    gated_grad = rgate * scaled - gated * rgate**3 * (cross / inner_all)[..., None]
    (
        inner_back,
        bmat_grad,
        cmat_grad,
        step_back,
        gate_back,
        grad_conv_weight,
        grad_conv_offset,
        grad_step_offset,
        grad_decay_log,
        grad_skip_gain,
    ) = mix_back(gated_grad)
    bmat_grad, cmat_grad = lax.psum((bmat_grad, cmat_grad), "tensor")
    bc_back_pre, grad_conv_bc_weight, grad_conv_bc_offset = bc_back((bmat_grad, cmat_grad))
    joint_gradient = jnp.concatenate([gate_back, inner_back], axis=-1).astype(jnp.bfloat16)
    stepsize_gradient = step_back.astype(jnp.bfloat16)
    state_input_gradient = bc_back_pre.astype(jnp.bfloat16)
    normed_part = jnp.einsum(
        "ugh,ih->ugi", joint_gradient, joint_matrix, preferred_element_type=jnp.float32
    )
    normed_part = normed_part + jnp.einsum(
        "ugh,ih->ugi", stepsize_gradient, stepsize_matrix, preferred_element_type=jnp.float32
    )
    normed_grad = lax.psum(normed_part, "tensor")
    normed_grad = normed_grad + jnp.einsum(
        "ugh,ih->ugi", state_input_gradient, state_input_matrix, preferred_element_type=jnp.float32
    )
    grad_norm_gain = jnp.sum(normed_grad * normal_hat, axis=(0, 1))
    lifted = normed_grad * norm_gain
    dealt_grad = inv_rms * (
        lifted - normal_hat * jnp.mean(lifted * normal_hat, axis=-1, keepdims=True)
    )
    input_dealt = (cot_float + dealt_grad).astype(jnp.bfloat16)
    returned = partner_2(input_dealt[1:], "dp", top_bit)
    tokens_grad = jnp.concatenate(
        [input_dealt[:1], jnp.where(moved[1], returned, input_dealt[1:])], axis=0
    )
    joint_weight = jnp.einsum(
        "ika,ikt->at", normalized_rows, joint_gradient, preferred_element_type=jnp.float32
    )
    stepsize_weight = jnp.einsum(
        "ika,ikt->at", normalized_rows, stepsize_gradient, preferred_element_type=jnp.float32
    )
    state_input_weight = jnp.einsum(
        "ika,ikt->at", normalized_rows, state_input_gradient, preferred_element_type=jnp.float32
    )
    grad_proj_gate, grad_proj_inner, grad_proj_step, grad_proj_bc, grad_proj_out = (
        lax.psum_scatter(joint_weight[:, :inner_dev], "dp", scatter_dimension=0, tiled=True),
        lax.psum_scatter(joint_weight[:, inner_dev:], "dp", scatter_dimension=0, tiled=True),
        lax.psum_scatter(stepsize_weight, "dp", scatter_dimension=0, tiled=True),
        lax.psum_scatter(state_input_weight, "dp", scatter_dimension=0, tiled=True),
        lax.psum_scatter(grad_proj_out, "dp", scatter_dimension=1, tiled=True),
    )
    (
        grad_norm_gain,
        grad_conv_weight,
        grad_conv_offset,
        grad_conv_bc_weight,
        grad_conv_bc_offset,
        grad_step_offset,
        grad_decay_log,
        grad_skip_gain,
        grad_out_gain,
    ) = lax.psum(
        (
            grad_norm_gain,
            grad_conv_weight,
            grad_conv_offset,
            grad_conv_bc_weight,
            grad_conv_bc_offset,
            grad_step_offset,
            grad_decay_log,
            grad_skip_gain,
            grad_out_gain,
        ),
        "dp",
    )
    return (
        block_out,
        tokens_grad,
        grad_norm_gain,
        grad_proj_gate,
        grad_proj_inner,
        grad_proj_bc,
        grad_proj_step,
        grad_conv_weight,
        grad_conv_offset,
        grad_conv_bc_weight,
        grad_conv_bc_offset,
        grad_step_offset,
        grad_decay_log,
        grad_skip_gain,
        grad_out_gain,
        grad_proj_out,
    )


def solution(mesh):
    return jax.shard_map(
        body,
        mesh=mesh,
        in_specs=(
            P("dp", None, None),
            P("dp", None, None),
            P(),
            P(),
            P(),
            P(None, "tensor"),
            P(None, "tensor"),
            P(),
            P(None, "tensor"),
            P(None, "tensor"),
            P("tensor"),
            P(),
            P(),
            P("tensor"),
            P("tensor"),
            P("tensor"),
            P("tensor"),
            P("tensor", None),
        ),
        out_specs=(
            P("dp", None, None),
            P("dp", None, None),
            P(),
            P("dp", "tensor"),
            P("dp", "tensor"),
            P("dp", None),
            P("dp", "tensor"),
            P(None, "tensor"),
            P("tensor"),
            P(),
            P(),
            P("tensor"),
            P("tensor"),
            P("tensor"),
            P("tensor"),
            P("tensor", "dp"),
        ),
        check_vma=False,
    )
```

profile of v0, /device:TPU:0, one launch (start us, length us, event | category | flops | bytes accessed | tf_op | source)
XLA Modules:
  0.0 833.5 jit_solution(940849701978738776)
XLA Ops:
  8.1 2.7 slice.101
  10.8 4.0 collective-permute-start
  17.9 65.4 %collective-permute-done = bf16[1,1024,768]{2,1,0:T(8,128)(2,1)} collective-permute-done((bf16[1,1024,768]{2,1,0:T(8,128)(2,1)}, bf16[1,1024,768]{2,1,0:T(8,128)(2,1)}, u32[]{:S(2)}, u32[]{:S(2)}) %collective-permute-start) | collective-permute-done | bytes 1572896 | tf_op jit(solution)/shard_map/ppermute | solution.py:16
  83.3 2.8 fusion.143
  88.9 14.5 %reduce-window.14 = f32[2,4,6,2,128]{4,3,2,1,0:T(2,128)S(1)} reduce-window(f32[2,4,6,2,128]{4,3,2,1,0:T(2,128)S(1)} %reshape.310, f32[]{:T(128)} %constant.111.clone.1), window={size=1x1x1x1x128 pad=0_0x0_0x0_0x0_0x127_0}, to_apply=%region_1.2 | reduce-window | flops 1560576 | bytes 98308 | tf_op jit(solution)/shard_map/reduce-window
  104.9 4.8 fusion.97
  109.9 2.4 copy-done.16
  112.4 3.7 fusion.41
  116.0 3.6 copy.263
  119.6 5.2 reshape.269
  124.8 2.7 fusion.103
  127.6 2.6 fusion.65
  132.9 4.3 fusion.84
  137.2 2.0 broadcast.151.clone
  139.2 11.9 %while.34 = (s32[]{:T(128)}, f32[2,6,128,64]{3,2,1,0:T(8,128)S(1)}, f32[4,2,6,128,64]{4,3,2,1,0:T(8,128)}, f32[4,2,6,1,1]{2,1,4,3,0:T(2,128)}, f32[4,2,6]{2,0,1:...) while((s32[]{:T(128)}, f32[2,6,128,64]{3,2,1,0:T(8,128)S(1)}, ...), condition=%wide.region_4.5_spmd.clone, body=%wide.region_3.4_spmd.clone.sunk | while | flops 393219 | bytes 3934504 | solution.py:60
  151.1 3.7 copy.279
  154.8 4.7 fusion.148
  162.9 14.5 %bitcast_add_fusion.3 = f32[2,4,256,6,64]{2,4,3,1,0:T(8,128)S(1)} fusion(f32[2,4,256,6,64]{2,4,3,1,0:T(8,128)S(1)} %bitcast.203, f32[2,4,6,256]{3,2,1,0:T(8,128)S(1)} %bitcast.211, f32[2,4,256,256]{3,2,1,0:T(8,128)S(1)} %fusion.147, f32[2,4,6,256]{3,2,1,0:T(8,128)S(1)} %copy-done.34, pred[256,256]{1,0:T(8,128)(4,1)S(1)} %copy-done.36, ...), kind=kOutput, calls=%fused_computation.65 | convolution fusion | flops 2430074880 | bytes 11747328 | tf_op jit(solution)/shard_map/jvp(sbhqk,sbkhp->sbqhp)/dot_general | solution.py:55
  177.5 3.7 copy.281
  181.2 5.2 reshape.275
  186.4 3.6 copy.282
  190.1 5.8 multiply_reduce_fusion.11
  195.8 5.9 psum.105
  201.8 7.2 multiply_reduce_fusion.3
  209.0 6.6 psum.107
  215.6 9.1 %multiply_reduce_fusion.4 = (f32[384]{0:T(512)}, f32[2,1024,384]{2,1,0:T(8,128)}, bf16[2,1024,384]{2,1,0:T(8,128)(2,1)}) fusion(f32[2,1024,384]{2,1,0:T(8,128)} %get-tuple-element.387, f32[2,1024,768]{2,1,0:T(8,128)} %copy-done.16, f32[2,1024]{1,0:T(2,128)S(1)} %broadcast_multiply_fusion.9, f32[2,1024,384]{2,1,0:T(8,128)} %get-tuple-element.385, ...), kind=kLoop, calls=%fused_computation.68 | loop fusion | flops 20446848 | bytes 20476416 | tf_op jit(solution)/shard_map/transpose(jvp())/reduce_sum | solution.py:87
  224.7 3.6 copy.283
  228.2 5.5 reshape.276
  233.8 8.8 %fusion.90 = f32[2,4,256,128]{3,2,1,0:T(8,128)} fusion(f32[2,4,6,128,64]{3,4,2,1,0:T(8,128)} %copy.279, f32[2,4,256,6,64]{2,1,4,3,0:T(4,128)} %reshape.276, f32[2,4,256,6]{2,3,1,0:T(8,128)S(1)} %copy-done.32), kind=kOutput, calls=%fused_computation.144 | convolution fusion | flops 1208745984 | bytes 5816320 | tf_op jit(solution)/shard_map/transpose(jvp(sbqn,sbhnp->sbqhp))/dot_general | solution.py:64
  242.6 2.9 multiply_reduce_fusion.9
  245.5 4.5 fusion.100
  250.0 4.3 fusion.83
  254.3 2.0 broadcast.151
  256.4 17.4 %while.35 = (s32[]{:T(128)}, f32[2,6,128,64]{3,2,1,0:T(8,128)S(1)}, f32[4,2,6]{2,0,1:T(4,128)S(1)}, f32[4,2,6,128,64]{4,3,2,1,0:T(8,128)}, f32[4,2,6,128,64]{3,4...) while((s32[]{:T(128)}, f32[2,6,128,64]{3,2,1,0:T(8,128)S(1)}, ...), condition=%wide.region_12.13_spmd.clone, body=%wide.region_10.12_spmd.clone.sunk | while | flops 589816 | bytes 4325808 | solution.py:60
  273.8 12.6 %fusion.91 = f32[2,4,256,128]{3,2,1,0:T(8,128)S(1)} fusion(f32[2,4,256,6,64]{2,1,4,3,0:T(4,128)} %reshape.269, f32[2,4,256,6]{2,3,1,0:T(8,128)S(1)} %get-tuple-element.414, f32[4,2,6,128,64]{4,3,2,1,0:T(8,128)} %get-tuple-element.193), kind=kOutput, calls=%fused_computation.145 | convolution fusion | flops 1208745984 | bytes 5816320 | tf_op jit(solution)/shard_map/transpose(jvp(sbhk,sbkn,sbkhp->sbhnp))/dot_general | solution.py:58
  286.5 5.5 multiply_reduce_fusion.2
  292.1 21.7 %fusion.12 = (f32[2,4,6,256]{3,2,1,0:T(8,128)}, f32[2,4,6,256]{3,2,1,0:T(8,128)}, f32[2,4,6,256]{3,2,1,0:T(8,128)}, f32[2,4,256,256]{3,2,1,0:T(8,128)}) fusion(f32[2,4,6,256]{3,2,1,0:T(8,128)S(1)} %bitcast.212, f32[2,4,256,256]{3,2,1,0:T(8,128)S(1)} %copy-done.29, f32[2,4,6,256]{3,2,1,0:T(8,128)S(1)} %copy-done.35, pred[256,256]{1,0:T(8,128)(4,1)S(1)} %copy-done.37, ...), kind=kOutput, calls=%fused_computation.28 | convolution fusion | flops 2456252416 | bytes 10797056 | tf_op jit(solution)/shard_map/transpose(jvp(sbhqk,sbkhp->sbqhp))/dot_general | solution.py:55
  313.8 11.3 %bitcast_add_fusion.2 = f32[2,4,256,6,64]{2,4,3,1,0:T(8,128)S(1)} fusion(f32[2,4,256,6,64]{2,4,3,1,0:T(8,128)S(1)} %get-tuple-element.428, f32[2,4,6,256]{3,2,1,0:T(8,128)S(1)} %bitcast.213, f32[2,4,256,256]{3,2,1,0:T(8,128)S(1)} %copy-done.29, f32[2,4,6,256]{3,2,1,0:T(8,128)S(1)} %copy-done.35, pred[256,256]{1,0:T(8,128)(4,1)S(1)} %copy-done.37, ...), kind=kOutput, calls=%fused_computation.64 | convolution fusion | flops 2430074880 | bytes 11747328 | tf_op jit(solution)/shard_map/transpose(jvp(sbhqk,sbkhp->sbqhp))/dot_general | solution.py:55
  325.1 4.1 copy.288
  329.3 5.3 reshape.277
  334.5 3.5 copy.289
  338.1 9.9 %multiply_reduce_fusion.7 = (f32[384]{0:T(512)}, f32[384]{0:T(512)}, f32[384]{0:T(512)}, f32[384]{0:T(512)}, f32[384]{0:T(512)}, /*index=5*/f32[2,1024,384]{2,1,0:T(8,128)S(1)}) fusion(f32[2,1024,384]{2,1,0:T(8,128)} %copy-done.8, f32[2,1024,768]{2,1,0:T(8,128)} %copy-done.16, f32[2,1024,384]{2,1,0:T(8,128)} %get-tuple-element.387, ...), kind=kLoop, calls=%fused_computation.71 | loop fusion | flops 15726720 | bytes 18883584 | tf_op jit(solution)/shard_map/transpose(jvp())/reduce_sum | solution.py:25
  348.0 5.0 broadcast_multiply_fusion
  353.0 3.0 convolution_add_fusion.3
  356.0 4.5 convolution_add_fusion.2
  361.8 60.5 %reduce-window.16 = f32[2,4,6,2,128]{4,3,2,1,0:T(2,128)S(1)} reduce-window(f32[2,4,6,2,128]{4,3,2,1,0:T(2,128)S(1)} %reshape.311, f32[]{:T(128)} %constant.111.clone.1), window={size=1x1x1x1x128 pad=0_0x0_0x0_0x0_0x0_127}, to_apply=%region_18.19 | reduce-window | flops 1560576 | bytes 98308 | tf_op jit(solution)/shard_map/reduce-window.2
  422.9 2.8 pad_add_fusion.6
  426.0 5.8 fusion.39
  431.9 2.6 fusion.67
  434.5 3.6 convolution_add_fusion.1
  439.6 3.6 convolution_bitcast_fusion.1
  443.1 7.8 fusion.76
  451.0 3.2 fusion.144
  454.8 6.2 fusion.87
  461.1 233.3 %all-reduce.25.cloned.1.call-done = (f32[2,1024,768]{2,1,0:T(8,128)}, f32[2,1024,768]{2,1,0:T(8,128)}, f32[2,1024,256]{2,1,0:T(8,128)}) async-done(((f32[2,1024,768]{2,1,0:T(8,128)}, f32[2,1024,768]{2,1,0:T(8,128)}, f32[2,1024,256]{2,1,0:T(8,128)}), (f32[2,1024,768]{2,1,0:T(8,128)}, f32[2,1024,768]{2,1,0:T(8,128)}, f32[2,1024,256]{2,1,0:T(8,128)})) %all-reduce.25.cloned.1.call-update) | async-done | bytes 14680080 | tf_op jit(solution)/shard_map/psum | solution.py:159
  694.4 6.3 multiply_reduce_fusion.15
  702.9 4.6 fusion.19
  707.9 3.7 fusion.18
  714.6 2.5 collective-permute-start.1
  717.1 2.3 convolution_bitcast_fusion
  721.3 94.4 %all-reduce.21 = (f32[768]{0:T(1024)}, f32[4,384]{1,0:T(4,128)}, f32[384]{0:T(512)}, f32[4,256]{1,0:T(4,128)}, f32[256]{0:T(256)}, /*index=5*/f32[6]{0:T(128)}, f32[6]{0:T(128)}, f32[6]{0:T(128)}, f32[384]{0:T(512)}) all-reduce(f32[768]{0:T(1024)S(1)} %get-tuple-element.322, ...), channel_id=1, replica_groups=mesh['dp'=8,'tensor'=4] {'dp'}, use_global_device_ids=true, to_apply=%region_26.27 | all-reduce | flops 4370 | bytes 34960 | tf_op jit(solution)/shard_map/psum | solution.py:236
  815.7 2.8 fusion.142
  818.5 1.9 pad_maximum_fusion.2
  820.4 5.2 reduce-scatter.12.cloned.1.call-done
  (311 shorter events, 54.5 us)
Async XLA Ops:
  8.0 193.7 %copy-start = (bf16[384,768]{1,0:T(8,128)(2,1)S(1)}, bf16[384,768]{1,0:T(8,128)(2,1)}, u32[]{:S(2)}) copy-start(bf16[384,768]{1,0:T(8,128)(2,1)} %param.39) | copy-start | bytes 1769476
  8.0 6.9 copy-start.79
  8.0 7.5 copy-start.78
  8.1 7.8 copy-start.2
  8.1 8.4 %copy-start.67 = (f32[4,384]{1,0:T(4,128)S(1)}, f32[4,384]{1,0:T(4,128)}, u32[]{:S(2)}) copy-start(f32[4,384]{1,0:T(4,128)} %param.31) | copy-start | bytes 18436
  8.1 9.1 %copy-start.86 = (f32[6]{0:T(128)S(1)}, f32[6]{0:T(128)}, u32[]{:S(2)}) copy-start(f32[6]{0:T(128)} %param.36) | copy-start | bytes 76
  8.1 9.1 %copy-start.70 = (f32[4,256]{1,0:T(4,128)S(1)}, f32[4,256]{1,0:T(4,128)}, u32[]{:S(2)}) copy-start(f32[4,256]{1,0:T(4,128)} %param.33) | copy-start | bytes 12292
  8.1 686.3 %all-reduce.25.cloned.1.call-start = ((), (), s32[]{:S(2)}) async-start(), calls=%async_computation.10 | async-start | bytes 29360128 | tf_op jit(solution)/shard_map/psum | solution.py:159
  10.8 72.4 %collective-permute-start = (bf16[1,1024,768]{2,1,0:T(8,128)(2,1)}, bf16[1,1024,768]{2,1,0:T(8,128)(2,1)}, u32[]{:S(2)}, u32[]{:S(2)}) collective-permute-start(bf16[1,1024,768]{2,1,0:T(8,128)(2,1)} %slice.101), channel_id=1, source_target_pairs={{0,16},{4,20},{8,24},{12,28},{16,0},{20,4},{24,8},{28,12},{1,17},{... | collective-permute-start | bytes 4718600 | tf_op jit(solution)/shard_map/ppermute | solution.py:16
  16.5 95.9 %copy-start.41 = (f32[384]{0:T(512)}, f32[384]{0:T(512)S(1)}, u32[]{:S(2)}) copy-start(f32[384]{0:T(512)S(1)} %get-tuple-element.336) | copy-start | bytes 4612
  16.5 95.8 %copy-start.43 = (f32[384]{0:T(512)}, f32[384]{0:T(512)S(1)}, u32[]{:S(2)}) copy-start(f32[384]{0:T(512)S(1)} %get-tuple-element.337) | copy-start | bytes 4612
  16.5 95.8 %copy-start.45 = (f32[384]{0:T(512)}, f32[384]{0:T(512)S(1)}, u32[]{:S(2)}) copy-start(f32[384]{0:T(512)S(1)} %get-tuple-element.338) | copy-start | bytes 4612
  16.5 95.8 %copy-start.47 = (f32[384]{0:T(512)}, f32[384]{0:T(512)S(1)}, u32[]{:S(2)}) copy-start(f32[384]{0:T(512)S(1)} %get-tuple-element.339) | copy-start | bytes 4612
  17.2 71.6 %copy-start.74 = (f32[6]{0:T(128)}, f32[6]{0:T(128)S(1)}, u32[]{:S(2)}) copy-start(f32[6]{0:T(128)S(1)} %exponential_negate_fusion) | copy-start | bytes 76
  17.2 110.4 %copy-start.53 = (f32[1,256]{1,0:T(1,128)}, f32[1,256]{1,0:T(1,128)S(1)}, u32[]{:S(2)}) copy-start(f32[1,256]{1,0:T(1,128)S(1)} %get-tuple-element.418) | copy-start | bytes 3076
  17.2 110.4 %copy-start.55 = (f32[1,256]{1,0:T(1,128)}, f32[1,256]{1,0:T(1,128)S(1)}, u32[]{:S(2)}) copy-start(f32[1,256]{1,0:T(1,128)S(1)} %get-tuple-element.419) | copy-start | bytes 3076
  17.2 110.4 %copy-start.57 = (f32[1,256]{1,0:T(1,128)}, f32[1,256]{1,0:T(1,128)S(1)}, u32[]{:S(2)}) copy-start(f32[1,256]{1,0:T(1,128)S(1)} %get-tuple-element.420) | copy-start | bytes 3076
  17.3 110.4 %copy-start.59 = (f32[1,256]{1,0:T(1,128)}, f32[1,256]{1,0:T(1,128)S(1)}, u32[]{:S(2)}) copy-start(f32[1,256]{1,0:T(1,128)S(1)} %get-tuple-element.421) | copy-start | bytes 3076
  86.9 18.0 %copy-start.80 = (bf16[768,384]{1,0:T(8,128)(2,1)S(1)}, bf16[768,384]{1,0:T(8,128)(2,1)}, u32[]{:S(2)}) copy-start(bf16[768,384]{1,0:T(8,128)(2,1)} %param.28) | copy-start | bytes 1769476
  119.6 5.2 copy-start.83
  131.4 7.9 copy-start.11
  159.5 18.0 %copy-start.22 = (f32[2,4,256,384]{2,3,1,0}, f32[2,4,256,384]{2,3,1,0:S(1)}, u32[]{:S(2)}) copy-start(f32[2,4,256,384]{2,3,1,0:S(1)} %fusion.148) | copy-start | bytes 9437188
  161.4 16.1 %copy-start.28 = (f32[2,4,256,256]{3,2,1,0:T(8,128)}, f32[2,4,256,256]{3,2,1,0:T(8,128)S(1)}, u32[]{:S(2)}) copy-start(f32[2,4,256,256]{3,2,1,0:T(8,128)S(1)} %fusion.147) | copy-start | bytes 6291460
  190.0 11.7 %copy-start.40 = (f32[384]{0:T(512)S(1)}, f32[384]{0:T(512)}, u32[]{:S(2)}) copy-start(f32[384]{0:T(512)} %param.38) | copy-start | bytes 4612
  190.0 11.7 %copy-start.68 = (bf16[2,1024]{1,0:T(2,128)(2,1)S(1)}, bf16[2,1024]{1,0:T(2,128)(2,1)}, u32[]{:S(2)}) copy-start(bf16[2,1024]{1,0:T(2,128)(2,1)} %get-tuple-element.423) | copy-start | bytes 12292
  233.8 8.8 %copy-start.6 = (f32[2,4,256,6,64]{2,1,4,3,0:T(4,128)S(1)}, f32[2,4,256,6,64]{2,1,4,3,0:T(4,128)}, u32[]{:S(2)}) copy-start(f32[2,4,256,6,64]{2,1,4,3,0:T(4,128)} %reshape.276) | copy-start | bytes 9437188
  273.8 12.6 %copy-start.49 = (f32[4,2,6]{2,0,1:T(4,128)}, f32[4,2,6]{2,0,1:T(4,128)S(1)}, u32[]{:S(2)}) copy-start(f32[4,2,6]{2,0,1:T(4,128)S(1)} %get-tuple-element.194) | copy-start | bytes 580
  273.8 12.6 %copy-start.5 = (f32[2,4,256,6,64]{2,1,4,3,0:T(4,128)S(1)}, f32[2,4,256,6,64]{2,1,4,3,0:T(4,128)}, u32[]{:S(2)}) copy-start(f32[2,4,256,6,64]{2,1,4,3,0:T(4,128)} %reshape.269) | copy-start | bytes 9437188
  273.8 12.6 %copy-start.10 = (f32[4,2,6,128,64]{4,3,2,1,0:T(8,128)S(1)}, f32[4,2,6,128,64]{4,3,2,1,0:T(8,128)}, u32[]{:S(2)}) copy-start(f32[4,2,6,128,64]{4,3,2,1,0:T(8,128)} %get-tuple-element.193) | copy-start | bytes 4718596
  286.5 5.6 copy-start.7
  286.5 5.6 copy-start.29
  286.5 5.6 copy-start.35
  286.5 5.6 copy-start.37
  338.1 9.9 %copy-start.42 = (f32[384]{0:T(512)S(1)}, f32[384]{0:T(512)}, u32[]{:S(2)}) copy-start(f32[384]{0:T(512)} %copy-done.41) | copy-start | bytes 4612
  338.1 9.9 %copy-start.44 = (f32[384]{0:T(512)S(1)}, f32[384]{0:T(512)}, u32[]{:S(2)}) copy-start(f32[384]{0:T(512)} %copy-done.43) | copy-start | bytes 4612
  338.1 9.9 %copy-start.46 = (f32[384]{0:T(512)S(1)}, f32[384]{0:T(512)}, u32[]{:S(2)}) copy-start(f32[384]{0:T(512)} %copy-done.45) | copy-start | bytes 4612
  338.1 9.9 %copy-start.48 = (f32[384]{0:T(512)S(1)}, f32[384]{0:T(512)}, u32[]{:S(2)}) copy-start(f32[384]{0:T(512)} %copy-done.47) | copy-start | bytes 4612
  348.0 5.1 copy-start.24
  348.0 5.1 copy-start.25
  356.0 66.8 %copy-start.33 = (f32[2,1024,6]{1,2,0:T(8,128)S(1)}, f32[2,1024,6]{1,2,0:T(8,128)}, u32[]{:S(2)}) copy-start(f32[2,1024,6]{1,2,0:T(8,128)} %get-tuple-element.425) | copy-start | bytes 147460
  356.0 66.9 %copy-start.26 = (f32[2,4,256,128]{3,2,1,0:T(8,128)S(1)}, f32[2,4,256,128]{3,2,1,0:T(8,128)}, u32[]{:S(2)}) copy-start(f32[2,4,256,128]{3,2,1,0:T(8,128)} %convolution_add_fusion.3) | copy-start | bytes 3145732
  360.5 65.2 %copy-start.38 = (f32[2,4,6,256]{3,2,1,0:T(8,128)S(1)}, f32[2,4,6,256]{3,2,1,0:T(8,128)}, u32[]{:S(2)}) copy-start(f32[2,4,6,256]{3,2,1,0:T(8,128)} %get-tuple-element.320) | copy-start | bytes 147460
  360.5 65.2 %copy-start.75 = (f32[6]{0:T(128)S(1)}, f32[6]{0:T(128)}, u32[]{:S(2)}) copy-start(f32[6]{0:T(128)} %copy-done.74) | copy-start | bytes 76
  426.0 5.8 copy-start.30
  426.0 5.8 copy-start.81
  426.0 5.8 copy-start.82
  438.2 281.5 %reduce-scatter.16.cloned.1.call-start = ((), (), s32[]{:S(2)}) async-start(), calls=%async_computation.9 | async-start | bytes 442368
  450.9 369.5 %reduce-scatter.10.cloned.1.call-start = ((), (), s32[]{:S(2)}) async-start(), calls=%async_computation.6 | async-start | bytes 1327104 | tf_op jit(solution)/shard_map/reduce_scatter | solution.py:221
  454.2 366.2 %reduce-scatter.8.cloned.1.call-start = ((), (), s32[]{:S(2)}) async-start(), calls=%async_computation.5 | async-start | bytes 1327104 | tf_op jit(solution)/shard_map/reduce_scatter | solution.py:220
  454.8 365.7 %reduce-scatter.14.cloned.1.call-start = ((), (), s32[]{:S(2)}) async-start(), calls=%async_computation.8 | async-start | bytes 1327104 | tf_op jit(solution)/shard_map/reduce_scatter | solution.py:224
  461.0 364.6 %reduce-scatter.12.cloned.1.call-start = ((), (), s32[]{:S(2)}) async-start(), calls=%async_computation.7 | async-start | bytes 884736 | tf_op jit(solution)/shard_map/reduce_scatter | solution.py:223
  694.4 6.3 copy-start.54
  694.4 6.3 copy-start.56
  694.4 6.3 copy-start.58
  694.4 6.3 copy-start.60
  702.2 5.3 slice-start
  702.9 5.0 copy-start.27
  702.9 5.0 copy-start.39
  714.5 4.9 copy-start.61
  714.6 5.1 copy-start.87
  714.6 6.7 copy-start.66
  714.6 6.7 copy-start.76
  714.6 101.1 %collective-permute-start.1 = (bf16[1,1024,768]{2,1,0:T(8,128)(2,1)}, bf16[1,1024,768]{2,1,0:T(8,128)(2,1)}, u32[]{:S(2)}, u32[]{:S(2)}) collective-permute-start(bf16[1,1024,768]{2,1,0:T(8,128)(2,1)} %slice.141), channel_id=1, source_target_pairs={{0,16},{4,20},{8,24},{12,28},{16,0},{20,4},{24,8},{28,12},{1,17},{... | collective-permute-start | bytes 4718600 | tf_op jit(solution)/shard_map/ppermute | solution.py:16
  818.5 7.2 copy-start.1
  (34 other events, 103.6 us)
Sparse Core Ops, SparseCore 0:
  438.3 255.9 all-reduce.24
Sparse Core Ops, SparseCore 1:
  451.0 62.3 reduce-scatter.15
  517.2 63.0 reduce-scatter.9
  584.1 63.1 reduce-scatter.7
  651.3 63.0 reduce-scatter.13
  719.5 106.1 reduce-scatter.11
where the time goes:
time: 845 us; the launch traced here: 834 us
  waiting for transfers between devices  305 us (36%)
  other arithmetic  160 us (19%)
  matrix products  149 us (18%)
  blocking collectives  107 us (13%)
  local copies, waits for them, and re-layouts  89.4 us (11%)
  between operations  17.1 us (2%)
    psum x1, waiting for transfers between devices, body(): branch = lax.psum(partial_out, 'tensor')  233 us
    psum x1, blocking collectives, body(): lax.psum((grad_norm_gain, grad_conv_weight, grad_conv_offset, grad_conv_b...  94.4 us
    another operation x8, other arithmetic  81.7 us
    ppermute x2, waiting for transfers between devices, partner_2(): return lax.ppermute(value, axis, pairs)  65.4 us
    dot_general x3, matrix products, block_scan(): inside = jnp.einsum('sbhqk,sbkhp->sbqhp', mixing, vblock, precision=HIGH)  47.6 us
    dot_general x3, matrix products, block_scan(): jnp.einsum('sbhk,sbkn,sbkhp->sbhnp', to_end, bblock, vblock, precision=HIGH)  22.4 us
  transfers between devices with their start and end apart: 8, of which 3 were waited for; matrix products, arithmetic and copies ran while one was open for 6% of the time, Pallas kernels for 0%

commit v1 on v0

v1 whole, which is shorter than its diff:
```python
import functools

import numpy as np
import jax
import jax.numpy as jnp
from jax import lax
from jax.experimental import pallas as pl
from jax.experimental.pallas import tpu as pltpu
from jax.sharding import PartitionSpec as P

EPS = 1e-05
SUB = 128
ROWS = 256
HP = 8
F32 = jnp.float32
BF = jnp.bfloat16
HIGH = lax.Precision.HIGHEST
NT = (((1,), (1,)), ((), ()))
TN = (((0,), (0,)), ((), ()))


def dot(a, b, dims=(((1,), (0,)), ((), ())), precision=None):
    return lax.dot_general(a, b, dims, precision=precision, preferred_element_type=F32)


def sigmoid(v):
    return 1.0 / (1.0 + jnp.exp(-v))


def split(v):
    high = v.astype(BF).astype(F32)
    return high, (v - high).astype(BF).astype(F32)


def spread_matrix(heads, hsize, kinds):
    inner = heads * hsize
    out = np.zeros((2, kinds, HP, kinds, heads, hsize), np.float32)
    for kind in range(kinds):
        for head in range(heads):
            out[:, kind, head, kind, head] = 1
    return out.reshape(2 * kinds * HP, kinds * inner)


def gather_matrix(heads, hsize):
    inner = heads * hsize
    out = np.zeros((4, heads, hsize, 128), np.float32)
    for part, base in enumerate((0, 0, HP, 2 * HP)):
        for head in range(heads):
            out[part, head, :, base + head] = 1
    return out.reshape(4 * inner, 128)


def spread(rows, matrix):
    parts = [split(r) for r in rows]
    stack = jnp.concatenate([p[0] for p in parts] + [p[1] for p in parts], axis=0)
    wide = dot(stack.T.astype(BF), matrix)
    inner = wide.shape[1] // len(rows)
    return [wide[:, k * inner : (k + 1) * inner] for k in range(len(rows))]


def pair_blocks(values, low_lanes):
    zero = jnp.zeros_like(values)
    return jnp.concatenate([jnp.where(low_lanes, values, zero), jnp.where(low_lanes, zero, values)], axis=0)


def fwd_kernel(
    tok_ref, gain_ref, w_ref, wst_ref, cw_ref, cb_ref, hp_ref, skip_ref, og_ref, wout_ref, spread_ref,
    p_ref, sq_ref, sg_ref, gy_ref, gated_ref, yi_ref, yo_ref, x_ref, xs_ref, bc_ref, dsil_ref, pre_ref,
    rows_ref, sin_ref, normed_ref,
    buf, state,
):
    rows = tok_ref.shape[0]
    inner = og_ref.shape[1]
    nstate = state.shape[0]
    wide = buf.shape[1]
    heads = inner // 64

    @pl.when(pl.program_id(0) == 0)
    def _():
        state[...] = jnp.zeros_like(state)
        buf[0:8, :] = jnp.zeros((8, wide), F32)

    tok = tok_ref[...].astype(F32)
    rstd = lax.rsqrt(jnp.mean(tok * tok, axis=-1, keepdims=True) + EPS)
    normed = (tok * rstd * gain_ref[...]).astype(BF)
    normed_ref[...] = normed
    pre = dot(normed, w_ref[...])
    gate_pre = pre[:, :inner]
    buf[8 : 8 + rows, :] = pre[:, inner:]
    pre_ref[...] = pre[:, inner:].astype(pre_ref.dtype)
    step_pre = dot(wst_ref[...], normed, NT) + hp_ref[:, 0:1]
    steps = jnp.maximum(step_pre, 0.0) + jnp.log1p(jnp.exp(-jnp.abs(step_pre)))
    rows_ref[0:HP, :] = steps
    rows_ref[2 * HP : 3 * HP, :] = sigmoid(step_pre)
    rates = steps * hp_ref[:, 1:2]

    conv = cb_ref[...] + cw_ref[0:1, :] * buf[5 : 5 + rows, :]
    for tap in range(1, 4):
        conv = conv + cw_ref[tap : tap + 1, :] * buf[5 + tap : 5 + tap + rows, :]
    buf[0:8, :] = buf[rows : rows + 8, :]
    sig = sigmoid(conv)
    act = conv * sig
    dsil_ref[...] = (sig * (1.0 + conv * (1.0 - sig))).astype(dsil_ref.dtype)
    x = act[:, :inner]
    x_ref[...] = x.astype(x_ref.dtype)
    bc = act[:, inner:].astype(BF)
    bc_ref[...] = bc

    at_row = lax.broadcasted_iota(jnp.int32, (SUB, SUB), 0)
    at_col = lax.broadcasted_iota(jnp.int32, (SUB, SUB), 1)
    causal = at_row >= at_col
    upper = (at_row <= at_col).astype(F32)
    low_lanes = lax.broadcasted_iota(jnp.int32, (SUB, 128), 1) < 64
    gsig = sigmoid(gate_pre)
    sgate = gate_pre * gsig
    dgate = gsig * (1.0 + gate_pre * (1.0 - gsig))
    for sub in range(rows // SUB):
        here = slice(sub * SUB, (sub + 1) * SUB)
        cum = dot(rates[:, here], upper, precision=HIGH)
        rows_ref[HP : 2 * HP, here] = cum
        cum_col = cum.T
        step_x, ecum_x, eend_x = spread(
            [steps[:, here], jnp.exp(cum), jnp.exp(cum[:, SUB - 1 : SUB] - cum)], spread_ref[...]
        )
        bmat = bc[here, :nstate]
        cmat = bc[here, nstate:]
        xs = x[here] * step_x
        xsb = xs.astype(BF)
        xs_ref[here, :] = xsb
        scores = dot(cmat, bmat, NT)
        inside = []
        for pair in range(heads // 2):
            mix = []
            for head in (2 * pair, 2 * pair + 1):
                gap = cum_col[:, head : head + 1] - cum[head : head + 1, :]
                mix.append((jnp.exp(jnp.where(causal, gap, -1e30)) * scores).astype(BF))
            blocks = pair_blocks(xsb[:, pair * 128 : (pair + 1) * 128], low_lanes)
            inside.append(dot(jnp.concatenate(mix, axis=1), blocks))
        inside = jnp.concatenate(inside, axis=1)
        yi_ref[here, :] = inside
        enter = state[...]
        enter_b = enter.astype(BF)
        sin_ref[here, :] = enter_b
        outside = dot(cmat, enter_b) * ecum_x
        yo_ref[here, :] = outside.astype(yo_ref.dtype)
        xw = (xs * eend_x).astype(BF)
        state[...] = enter * ecum_x[SUB - 1 : SUB, :] + dot(bmat, xw, TN)
        y = inside + outside + skip_ref[...] * x[here]
        gated = y * sgate[here]
        gy_ref[here, :] = (y * dgate[here]).astype(gy_ref.dtype)
        gated_ref[here, :] = gated.astype(gated_ref.dtype)
        sq_ref[:, here] = dot(jnp.ones((HP, inner), BF), (gated * gated).astype(BF), NT)
        p_ref[here, :] = dot((gated * og_ref[...]).astype(BF), wout_ref[...]).astype(BF)
    sg_ref[...] = sgate.astype(sg_ref.dtype)


def mid_kernel(len_ref, cot_ref, gated_ref, sq_ref, og_ref, wout_ref, nog_ref, stat_ref):
    rows = cot_ref.shape[0]
    first = pl.program_id(0) * rows
    live = first + lax.broadcasted_iota(jnp.int32, (rows, 1), 0) < len_ref[0]
    branch_grad = jnp.where(live, cot_ref[...], jnp.zeros((), BF))
    nog = dot(branch_grad, wout_ref[...], NT)
    nog_ref[...] = nog.astype(nog_ref.dtype)
    inner = og_ref.shape[1]
    cross = nog * og_ref[...] * gated_ref[...].astype(F32)
    sums = dot(jnp.ones((HP, inner), BF), cross.astype(BF), NT)
    top = lax.broadcasted_iota(jnp.int32, (HP, rows), 0) == 0
    stat_ref[...] = jnp.where(top, sq_ref[...], sums)


def bwd_kernel(
    inner_all,
    len_ref, tok_ref, gain_ref, w_ref, wst_ref, cw_ref, hp_ref, skip_ref, og_ref, spread_ref, gather_ref,
    stat_ref, nog_ref, sg_ref, gy_ref, gated_ref, yi_ref, yo_ref, x_ref, xs_ref, bc_ref, dsil_ref, pre_ref,
    rows_ref, sin_ref,
    joint_ref, stepg_ref, n_ref, gnorm_ref, gconv_ref, ggain_ref, gog_ref, gskip_ref, ghead_ref,
    buf, dstate,
):
    rows = tok_ref.shape[0]
    inner = og_ref.shape[1]
    nstate = dstate.shape[0]
    wide = buf.shape[1]
    heads = inner // 64
    turn = pl.program_id(0)
    first = (pl.num_programs(0) - 1 - turn) * rows

    @pl.when(turn == 0)
    def _():
        dstate[...] = jnp.zeros_like(dstate)
        buf[rows : rows + 8, :] = jnp.zeros((8, wide), F32)
        for ref in (gconv_ref, ggain_ref, gog_ref, gskip_ref, ghead_ref):
            ref[...] = jnp.zeros_like(ref)

    at_row = lax.broadcasted_iota(jnp.int32, (SUB, SUB), 0)
    at_col = lax.broadcasted_iota(jnp.int32, (SUB, SUB), 1)
    causal_t = at_row <= at_col
    lower = (at_row >= at_col).astype(F32)
    upper_strict = (at_row < at_col).astype(F32)
    low_lanes = lax.broadcasted_iota(jnp.int32, (SUB, 128), 1) < 64
    last_row = lax.broadcasted_iota(jnp.int32, (SUB, 1), 0) == SUB - 1
    og = og_ref[...]
    skip = skip_ref[...]

    for sub in reversed(range(rows // SUB)):
        here = slice(sub * SUB, (sub + 1) * SUB)
        stat = stat_ref[:, here]
        rg = lax.rsqrt(stat[0:1, :] * (1.0 / inner_all) + EPS)
        coef = rg * rg * rg * stat[1:2, :] * (1.0 / inner_all)
        cols = jnp.concatenate([rg, coef, jnp.zeros((6, SUB), F32)], axis=0).T
        rgate = cols[:, 0:1]
        gated = gated_ref[here, :].astype(F32)
        nog = nog_ref[here, :].astype(F32)
        live = first + sub * SUB + lax.broadcasted_iota(jnp.int32, (SUB, 1), 0) < len_ref[0]
        ghat = gated * rgate
        gnorm_ref[here, :] = jnp.where(live, ghat * og, 0.0).astype(BF)
        gog_ref[0:1, :] += jnp.sum(nog * ghat, axis=0, keepdims=True)
        gg = rgate * (nog * og) - gated * cols[:, 1:2]
        joint_ref[here, :inner] = (gg * gy_ref[here, :].astype(F32)).astype(BF)
        dyb = (gg * sg_ref[here, :].astype(F32)).astype(BF)
        dy = dyb.astype(F32)

        steps = rows_ref[0:HP, here]
        cum = rows_ref[HP : 2 * HP, here]
        cum_col = cum.T
        step_x, ecum_x, eend_x = spread(
            [steps, jnp.exp(cum), jnp.exp(cum[:, SUB - 1 : SUB] - cum)], spread_ref[...]
        )
        bmat = bc_ref[here, :nstate]
        cmat = bc_ref[here, nstate:]
        xsb = xs_ref[here, :]
        xs = xsb.astype(F32)
        xf = x_ref[here, :].astype(F32)
        scores_t = dot(bmat, cmat, NT)
        dscores_t = jnp.zeros((SUB, SUB), F32)
        dxs_in = []
        for pair in range(heads // 2):
            lanes = slice(pair * 128, (pair + 1) * 128)
            mix = []
            dy_blocks = pair_blocks(dyb[:, lanes], low_lanes)
            for head in (2 * pair, 2 * pair + 1):
                gap = cum[head : head + 1, :] - cum_col[:, head : head + 1]
                weight = jnp.exp(jnp.where(causal_t, gap, -1e30))
                mix.append((weight * scores_t).astype(BF))
                part = head - 2 * pair
                dmix = dot(xsb[:, lanes], dy_blocks[part * SUB : (part + 1) * SUB, :], NT)
                dscores_t = dscores_t + dmix * weight
            dxs_in.append(dot(jnp.concatenate(mix, axis=1), dy_blocks))
        dxs_in = jnp.concatenate(dxs_in, axis=1)
        dleave = dstate[...]
        dleave_b = dleave.astype(BF)
        enter_b = sin_ref[here, :]
        xwb = (xs * eend_x).astype(BF)
        dye = (dy * ecum_x).astype(BF)
        dsc = dscores_t.astype(BF)
        dxw = dot(bmat, dleave_b)
        dbm = dot(dsc, cmat) + dot(xwb, dleave_b, NT)
        dcm = dot(dsc, bmat, TN) + dot(dye, enter_b, NT)
        dxs = dxs_in + eend_x * dxw
        dx = step_x * dxs + skip * dy
        gskip_ref[0:1, :] += jnp.sum(dy * xf, axis=0, keepdims=True)
        z1 = dy * (yi_ref[here, :] + yo_ref[here, :].astype(F32)) - xs * dxs_in
        ends = ecum_x[SUB - 1 : SUB, :]
        carry = jnp.sum(enter_b.astype(F32) * dleave, axis=0, keepdims=True) * ends
        z1 = z1 + jnp.where(last_row, carry, 0.0)
        z1h, z1l = split(z1)
        packed = jnp.concatenate(
            [z1h.astype(BF), z1l.astype(BF), (xwb.astype(F32) * dxw).astype(BF), (xf * dxs).astype(BF)], axis=1
        )
        sums = dot(packed, gather_ref[...]).T
        da = dot(sums[0:HP], lower, precision=HIGH) + dot(sums[HP : 2 * HP], upper_strict, precision=HIGH)
        dstate[...] = dleave * ends + dot(cmat, dye, TN)
        rate = hp_ref[:, 1:2]
        dstep_pre = (rate * da + sums[2 * HP : 3 * HP]) * rows_ref[2 * HP : 3 * HP, here]
        stepg_ref[:, here] = dstep_pre.astype(BF).astype(F32)
        ghead_ref[0:HP, :] += dstep_pre
        ghead_ref[HP : 2 * HP, :] += da * steps * rate
        buf[here, :inner] = dx * dsil_ref[here, :inner].astype(F32)
        buf[here, inner:] = jnp.concatenate([dbm, dcm], axis=1) * dsil_ref[here, inner:].astype(F32)

    pre = pre_ref[...].astype(F32)
    back = jnp.zeros((rows, wide), F32)
    for tap in range(4):
        moved = buf[3 - tap : 3 - tap + rows, :]
        back = back + cw_ref[tap : tap + 1, :] * moved
        gconv_ref[tap : tap + 1, :] += jnp.sum(moved * pre, axis=0, keepdims=True)
    gconv_ref[4:5, :] += jnp.sum(buf[0:rows, :], axis=0, keepdims=True)
    buf[rows : rows + 8, :] = buf[0:8, :]
    joint_ref[:, inner:] = back.astype(BF)
    grad = dot(joint_ref[...], w_ref[...], NT) + dot(stepg_ref[...].astype(BF), wst_ref[...], TN)
    n_ref[...] = grad.astype(BF)
    tok = tok_ref[...].astype(F32)
    hat = tok * lax.rsqrt(jnp.mean(tok * tok, axis=-1, keepdims=True) + EPS)
    ggain_ref[0:1, :] += jnp.sum(grad * hat, axis=0, keepdims=True)


def whole(shape):
    return pl.BlockSpec(shape, lambda i: (0,) * len(shape))


def down(shape, blocks=0):
    if blocks:
        return pl.BlockSpec(shape, lambda i: (blocks - 1 - i, 0))
    return pl.BlockSpec(shape, lambda i: (i, 0))


def across(shape, blocks=0):
    if blocks:
        return pl.BlockSpec(shape, lambda i: (0, blocks - 1 - i))
    return pl.BlockSpec(shape, lambda i: (0, i))


PARAMS = pltpu.CompilerParams(vmem_limit_bytes=48 * 1024 * 1024)


def forward(tok, gain, w, wst, cw, cb, hp, skip, og, wout, spread_m, nstate):
    length, width = tok.shape
    inner = og.shape[1]
    wide = cw.shape[1]
    sds = jax.ShapeDtypeStruct
    r = ROWS
    outs = [
        (sds((length, width), BF), down((r, width))),
        (sds((HP, length), F32), across((HP, r))),
        (sds((length, inner), F32), down((r, inner))),
        (sds((length, inner), F32), down((r, inner))),
        (sds((length, inner), F32), down((r, inner))),
        (sds((length, inner), F32), down((r, inner))),
        (sds((length, inner), F32), down((r, inner))),
        (sds((length, inner), F32), down((r, inner))),
        (sds((length, inner), BF), down((r, inner))),
        (sds((length, 2 * nstate), BF), down((r, 2 * nstate))),
        (sds((length, wide), F32), down((r, wide))),
        (sds((length, wide), F32), down((r, wide))),
        (sds((3 * HP, length), F32), across((3 * HP, r))),
        (sds((length, inner), BF), down((r, inner))),
        (sds((length, width), BF), down((r, width))),
    ]
    ins = [tok, gain, w, wst, cw, cb, hp, skip, og, wout, spread_m]
    return pl.pallas_call(
        fwd_kernel,
        grid=(length // r,),
        in_specs=[down((r, width))] + [whole(v.shape) for v in ins[1:]],
        out_specs=[o[1] for o in outs],
        out_shape=[o[0] for o in outs],
        scratch_shapes=[pltpu.VMEM((r + 8, wide), F32), pltpu.VMEM((nstate, inner), F32)],
        compiler_params=PARAMS,
        name="forward",
    )(*ins)


def middle(live, cot, gated, sq, og, wout):
    length, width = cot.shape
    inner = og.shape[1]
    r = ROWS
    return pl.pallas_call(
        mid_kernel,
        grid=(length // r,),
        in_specs=[
            pl.BlockSpec(memory_space=pltpu.SMEM), down((r, width)), down((r, inner)), across((HP, r)),
            whole(og.shape), whole(wout.shape),
        ],
        out_specs=[down((r, inner)), across((HP, r))],
        out_shape=[
            jax.ShapeDtypeStruct((length, inner), F32), jax.ShapeDtypeStruct((HP, length), F32),
        ],
        compiler_params=PARAMS,
        name="middle",
    )(live, cot, gated, sq, og, wout)


def backward(live, tok, gain, w, wst, cw, hp, skip, og, spread_m, gather_m, stat, nog, kept, inner_all):
    length, width = tok.shape
    inner = og.shape[1]
    wide = cw.shape[1]
    nstate = (wide - inner) // 2
    sg, gy, gated, yi, yo, x, xs, bc, dsil, pre, rowsv, sin = kept
    r = ROWS
    n = length // r
    sds = jax.ShapeDtypeStruct
    consts = [gain, w, wst, cw, hp, skip, og, spread_m, gather_m]
    tall = [nog, sg, gy, gated, yi, yo, x, xs, bc, dsil, pre]
    outs = [
        (sds((length, inner + wide), BF), down((r, inner + wide), n)),
        (sds((HP, length), F32), across((HP, r), n)),
        (sds((length, width), BF), down((r, width), n)),
        (sds((length, inner), BF), down((r, inner), n)),
        (sds((8, wide), F32), whole((8, wide))),
        (sds((8, width), F32), whole((8, width))),
        (sds((8, inner), F32), whole((8, inner))),
        (sds((8, inner), F32), whole((8, inner))),
        (sds((2 * HP, SUB), F32), whole((2 * HP, SUB))),
    ]
    return pl.pallas_call(
        functools.partial(bwd_kernel, inner_all),
        grid=(n,),
        in_specs=[pl.BlockSpec(memory_space=pltpu.SMEM), down((r, width), n)]
        + [whole(v.shape) for v in consts]
        + [across((HP, r), n)]
        + [down((r, v.shape[1]), n) for v in tall]
        + [across((3 * HP, r), n), down((r, inner), n)],
        out_specs=[o[1] for o in outs],
        out_shape=[o[0] for o in outs],
        scratch_shapes=[pltpu.VMEM((r + 8, wide), F32), pltpu.VMEM((nstate, inner), F32)],
        compiler_params=PARAMS,
        name="backward",
    )(live, tok, *consts, stat, *tall, rowsv, sin)


def swap(value, axis, bit):
    mask = 1 << bit
    return lax.ppermute(value, axis, [(i, i ^ mask) for i in range(lax.axis_size(axis))])


def bits(axis):
    return lax.axis_size(axis).bit_length() - 1


def sum_over(value, axis):
    for bit in range(bits(axis)):
        value = value + swap(value, axis, bit)
    return value


def half_of(value, which):
    size = value.shape[0] // 2
    return lax.dynamic_slice_in_dim(value, which * size, size, 0)


def join(mine, other, which):
    return jnp.where(which == 0, jnp.concatenate([mine, other], 0), jnp.concatenate([other, mine], 0))


def sum_half(partial, core):
    got = swap(half_of(partial, 1 - core), "tensor", 0)
    total = (half_of(partial, core).astype(F32) + got.astype(F32)).astype(BF)
    for bit in range(1, bits("tensor")):
        more = swap(total, "tensor", bit)
        if bit == bits("tensor") - 1:
            return total.astype(F32) + more.astype(F32)
        total = (total.astype(F32) + more.astype(F32)).astype(BF)


def scatter_rows(value):
    place = lax.axis_index("dp")
    nbits = bits("dp")
    rows = value.shape[0] >> nbits
    total = value.reshape((1 << nbits, rows) + value.shape[1:])
    for bit in range(nbits):
        mine = (place >> bit) & 1
        pairs = total.reshape((total.shape[0] // 2, 2) + total.shape[1:])
        keep = lax.dynamic_index_in_dim(pairs, mine, 1, keepdims=False)
        give = lax.dynamic_index_in_dim(pairs, 1 - mine, 1, keepdims=False)
        got = swap(give, "dp", bit)
        total = keep.astype(F32) + got.astype(F32)
        if bit < nbits - 1:
            total = total.astype(BF)
    return total[0]


def body(
    tokens, cotangent, lengths, perm, norm_gain, proj_gate, proj_inner, state_input_matrix, stepsize_matrix,
    conv_weight, conv_offset, conv_bc_weight, conv_bc_offset, step_offset, decay_log, skip_gain, out_gain,
    output_matrix,
):
    slots, length, width = tokens.shape
    inner = proj_gate.shape[1]
    heads = step_offset.shape[0]
    hsize = inner // heads
    nstate = state_input_matrix.shape[1] // 2
    inner_all = inner * lax.axis_size("tensor")
    place = lax.axis_index("dp")
    core = lax.axis_index("tensor") & 1
    top = bits("dp") - 1
    first = place * slots
    moved = lax.dynamic_index_in_dim(perm, first + 1, 0, keepdims=False) != first + 1

    w = jnp.concatenate([proj_gate, proj_inner, state_input_matrix], axis=1)
    wst = jnp.pad(stepsize_matrix.T, ((0, HP - heads), (0, 0)))
    cw = jnp.pad(jnp.concatenate([conv_weight, conv_bc_weight], axis=1), ((0, 4), (0, 0)))
    cb = jnp.concatenate([conv_offset, conv_bc_offset])[None]
    hp = jnp.pad(jnp.stack([step_offset, -jnp.exp(decay_log)], axis=1), ((0, HP - heads), (0, 126)))
    skip = jnp.repeat(skip_gain, hsize)[None]
    og = out_gain[None]
    gain = norm_gain[None]
    spread_m = jnp.asarray(spread_matrix(heads, hsize, 3), BF)
    gather_m = jnp.asarray(gather_matrix(heads, hsize), BF)

    far = swap(half_of(cotangent[1], core), "dp", top)
    near = swap(far, "tensor", 0)
    cots = [cotangent[0], jnp.where(moved, join(far, near, core), cotangent[1])]

    kept, partial, stats, nogs, lives = [], [], [], [], []
    for slot in range(slots):
        out = forward(tokens[slot], gain, w, wst, cw, cb, hp, skip, og, output_matrix, spread_m, nstate)
        partial.append(out[0])
        kept.append(out)
        live = lax.dynamic_slice_in_dim(lengths, first + slot, 1, 0)
        lives.append(live)
        nog, stat = middle(live, cots[slot], out[4], out[1], og, output_matrix)
        nogs.append(nog)
        stats.append(sum_over(stat, "tensor"))

    block_halves = []
    for slot in range(slots):
        branch = sum_half(partial[slot], core)
        rg = lax.rsqrt(half_of(stats[slot][0], core) / inner_all + EPS)
        mask = core * (length // 2) + jnp.arange(length // 2) < lives[slot][0]
        block = half_of(tokens[slot], core).astype(F32) + jnp.where(mask, rg, 0.0)[:, None] * branch
        block_halves.append(block.astype(BF))
    away = swap(block_halves[1], "dp", top)
    block_halves[1] = jnp.where(moved, away, block_halves[1])
    block_out = jnp.stack([join(b, swap(b, "tensor", 0), core) for b in block_halves])

    grads, results = [], []
    for slot in range(slots):
        res = backward(
            lives[slot], tokens[slot], gain, w, wst, cw, hp, skip, og, spread_m, gather_m, stats[slot], nogs[slot],
            kept[slot][2:14], inner_all,
        )
        results.append(res)
        normed_grad = sum_half(res[2], core)
        tok = half_of(tokens[slot], core).astype(F32)
        rstd = lax.rsqrt(jnp.mean(tok * tok, axis=-1, keepdims=True) + EPS)
        hat = tok * rstd
        lifted = normed_grad * norm_gain
        dealt_grad = rstd * (lifted - hat * jnp.mean(lifted * hat, axis=-1, keepdims=True))
        own = (half_of(cots[slot], core).astype(F32) + dealt_grad).astype(BF)
        grads.append(join(own, swap(own, "tensor", 0), core))
    tokens_grad = jnp.stack(grads)

    normed = jnp.concatenate([k[14] for k in kept], axis=0)
    joint = jnp.concatenate([r[0] for r in results], axis=0)
    gnorm = jnp.concatenate([r[3] for r in results], axis=0)
    cot_all = jnp.concatenate(cots, axis=0)
    stepg = jnp.concatenate([r[1] for r in results], axis=1).astype(BF)
    dw = dot(normed, joint, TN)
    dwo = dot(cot_all, gnorm, TN)
    dws = dot(stepg, normed).T
    packed = jnp.concatenate([dw, dwo, dws], axis=1).astype(BF)
    mine = scatter_rows(packed)
    wide = 2 * nstate
    small = [sum(r[k] for r in results) for k in range(4, 9)]
    gconv, ggain, gog, gskip, ghead = small
    ghead = jnp.sum(ghead, axis=1)
    gskip = jnp.sum(gskip[0].reshape(heads, hsize), axis=1)
    both = jnp.concatenate([ggain[0], gconv[:5, inner:].reshape(-1)])
    alone = jnp.concatenate(
        [gconv[:5, :inner].reshape(-1), gog[0], ghead[:heads], ghead[HP : HP + heads], gskip]
    )
    cut = both.shape[0]
    everything = sum_over(jnp.concatenate([both, alone]), "dp")
    bc_shard = mine[:, 2 * inner : 2 * inner + wide]
    summed = sum_over(jnp.concatenate([bc_shard.reshape(-1), everything[:cut]]), "tensor")
    both = summed[bc_shard.size :]
    alone = everything[cut:]
    conv_both = both[width:].reshape(5, wide)
    conv_own = alone[: 5 * inner].reshape(5, inner)
    tail = alone[5 * inner :]
    return (
        block_out,
        tokens_grad,
        both[:width],
        mine[:, :inner],
        mine[:, inner : 2 * inner],
        summed[: bc_shard.size].reshape(bc_shard.shape),
        mine[:, 3 * inner + wide : 3 * inner + wide + heads],
        conv_own[:4],
        conv_own[4],
        conv_both[:4],
        conv_both[4],
        tail[inner : inner + heads],
        tail[inner + heads : inner + 2 * heads],
        tail[inner + 2 * heads :],
        tail[:inner],
        mine[:, 2 * inner + wide : 3 * inner + wide].T,
    )


def solution(mesh):
    return jax.shard_map(
        body,
        mesh=mesh,
        in_specs=(
            P("dp", None, None), P("dp", None, None), P(), P(), P(), P(None, "tensor"), P(None, "tensor"), P(),
            P(None, "tensor"), P(None, "tensor"), P("tensor"), P(), P(), P("tensor"), P("tensor"), P("tensor"),
            P("tensor"), P("tensor", None),
        ),
        out_specs=(
            P("dp", None, None), P("dp", None, None), P(), P("dp", "tensor"), P("dp", "tensor"), P("dp", None),
            P("dp", "tensor"), P(None, "tensor"), P("tensor"), P(), P(), P("tensor"), P("tensor"), P("tensor"),
            P("tensor"), P("tensor", "dp"),
        ),
        check_vma=False,
    )
```

time: 845 us -> 282 us (0.33); the launches traced: 834 us -> 281 us
  waiting for transfers between devices: 305 us -> 84.9 us
  matrix products: 149 us -> 11.1 us
  other arithmetic: 160 us -> 37.9 us
  blocking collectives: 107 us -> 0 us
  Pallas kernels: 0 us -> 76.9 us
  local copies, waits for them, and re-layouts: 89.4 us -> 44.2 us
  starting transfers between devices: 6.79 us -> 23.5 us
  between operations: 17.1 us -> 2.09 us
    psum x1 -> x0, waiting for transfers between devices: 233 us -> none  [body(): branch = lax.psum(partial_out, 'tensor')]
    dot_general x23 -> x3, matrix products: 144 us -> 11.1 us  [dot(): lax.dot_general(a, b, dims, precision=precision, preferred_element_type=F32)]
    psum x3 -> x0, blocking collectives: 107 us -> none  [the longest x1 94.4 us: body(): lax.psum((grad_norm_gain, grad_conv_weight, grad_conv_offset, grad_conv_b...]
    another operation x8 -> x6, other arithmetic: 81.7 us -> 3.9 us  [the longest x1 1.94 us: body(): tokens_grad = jnp.stack(grads)]
    pallas_call x0 -> x6, Pallas kernels: none -> 76.9 us  [the longest x2 39.6 us: backward(): pl.pallas_call(functools.partial(bwd_kernel, inner_all), grid=(n,), in_sp...]
    reduce_sum x14 -> x5, other arithmetic: 40.7 us -> 3.17 us  [the longest x1 2.47 us: body(): jnp.mean(lifted * hat, axis=-1, keepdims=True)]
    reshape x7 -> x2, local copies, waits for them, and re-layouts: 28.4 us -> 0.01 us  [the longest x1 0.01 us: body(): both = jnp.concatenate([ggain[0], gconv[:5, inner:].reshape(-1)])]
    ppermute x2 -> x27, waiting for transfers between devices: 65.4 us -> 84.9 us  [swap(): lax.ppermute(value, axis, [(i, i ^ mask) for i in range(lax.axis_size(axi...]
  transfers between devices with their start and end apart: 8 -> 27, of which waited for: 3 -> 8; matrix products, arithmetic and copies ran while one was open for 6% -> 24% of each run, Pallas kernels for 0% -> 27%
where the time goes in v1:
time: 282 us; the launch traced here: 281 us
  waiting for transfers between devices  84.9 us (30%)
  Pallas kernels  76.9 us (27%)
  local copies, waits for them, and re-layouts  44.2 us (16%)
  other arithmetic  37.9 us (13%)
  starting transfers between devices  23.5 us (8%)
  matrix products  11.1 us (4%)
    ppermute x27, waiting for transfers between devices, swap(): lax.ppermute(value, axis, [(i, i ^ mask) for i in range(lax.axis_size(axi...  84.9 us
    pallas_call x2, Pallas kernels, backward(): pl.pallas_call(functools.partial(bwd_kernel, inner_all), grid=(n,), in_sp...  39.6 us
    pallas_call x2, Pallas kernels, forward(): pl.pallas_call(fwd_kernel, grid=(length // r,), in_specs=[down((r, width)...  31.5 us
    ppermute x27, starting transfers between devices, swap(): lax.ppermute(value, axis, [(i, i ^ mask) for i in range(lax.axis_size(axi...  23.5 us
    unnamed x138, local copies, waits for them, and re-layouts  20.2 us
    dot_general x3, matrix products, dot(): lax.dot_general(a, b, dims, precision=precision, preferred_element_type=F32)  11.1 us
    select_n x4, other arithmetic, join(): jnp.where(which == 0, jnp.concatenate([mine, other], 0), jnp.concatenate(...  7.97 us
    convert_element_type x4, other arithmetic, sum_half(): total = (half_of(partial, core).astype(F32) + got.astype(F32)).astype(BF)  6.48 us
  transfers between devices with their start and end apart: 27, of which 8 were waited for; matrix products, arithmetic and copies ran while one was open for 24% of the time, Pallas kernels for 27%

profile of v1, /device:TPU:0, one launch (start us, length us, event | category | flops | bytes accessed | tf_op | source)
XLA Modules:
  0.0 280.7 jit_solution(17042919801601719380)
XLA Ops:
  0.7 3.8 %fusion.60 = (bf16[1,1024,768]{2,1,0:T(8,128)(2,1)}, bf16[1024,768]{1,0:T(8,128)(2,1)}, bf16[1,1024,768]{2,1,0:T(8,128)(2,1)S(1)}) fusion(bf16[2,1024,768]{2,1,0:T(8,128)(2,1)} %param.21), kind=kLoop, calls=%fused_computation.114 | loop fusion | bytes 7864320 | tf_op jit(solution)/shard_map/slice | solution.py:490
  4.6 0.9 dynamic-slice_bitcast_fusion.1
  5.5 4.0 %collective-permute-start.5 = (bf16[512,768]{1,0:T(8,128)(2,1)}, bf16[512,768]{1,0:T(8,128)(2,1)}, u32[]{:S(2)}, u32[]{:S(2)}) collective-permute-start(bf16[512,768]{1,0:T(8,128)(2,1)} %dynamic-slice_bitcast_fusion.1), channel_id=1, source_target_pairs={{0,16},{4,20},{8,24},{12,28},{16,0},{20,4},{24,8},{28,12},{1,17},{... | collective-permute-start | bytes 2359304 | tf_op jit(solution)/shard_map/ppermute | solution.py:411
  9.9 0.9 constant_dynamic-update-slice_fusion.2
  10.9 0.9 constant_dynamic-update-slice_fusion.1
  12.6 4.8 %fusion.61 = (bf16[1,1024,768]{2,1,0:T(8,128)(2,1)}, bf16[1024,768]{1,0:T(8,128)(2,1)}, bf16[1024,768]{1,0:T(8,128)(2,1)}, bf16[1,1024,768]{2,1,0:T(8,128)(2,1)}) fusion(bf16[2,1024,768]{2,1,0:T(8,128)(2,1)} %param.20), kind=kLoop, calls=%fused_computation.115 | loop fusion | bytes 9437184 | tf_op jit(solution)/shard_map/slice | solution.py:508
  17.4 15.7 %forward.2 = (bf16[1024,768]{1,0:T(8,128)(2,1)S(1)}, f32[8,1024]{1,0:T(8,128)S(1)}, f32[1024,384]{1,0:T(8,128)S(1)}, f32[1024,384]{1,0:T(8,128)}, f32[1024,384]{...) custom-call(bf16[1024,768]{1,0:T(8,128)(2,1)} %get-tuple-element.174, ...), custom_call_target="tpu_custom_call" | custom-call | tf_op jit(solution)/shard_map/forward/pallas_call | solution.py:339
  33.1 1.1 copy-done.7
  35.7 1.2 copy-done.10
  36.9 0.9 constant_dynamic-slice_fusion.5
  38.5 1.4 copy-done.3
  39.9 2.8 %middle.2 = (f32[1024,384]{1,0:T(8,128)S(1)}, f32[8,1024]{1,0:T(8,128)S(1)}) custom-call(s32[1]{0:T(128)} %get-tuple-element.191.len_ref, bf16[1024,768]{1,0:T(8,128)(2,1)S(1)} %copy-done.3, f32[1024,384]{1,0:T(8,128)S(1)} %copy-done.2, f32[8,1024]{1,0:T(8,128)S(1)} %get-tuple-element.69.sq_ref, f32[1,384]{1,0:T(1,128)S(1)} %broadcast_in_dim.28.og_ref, ...), custom_call_target="tpu_custom_call" | custom-call | tf_op jit(solution)/shard_map/middle/pallas_call | solution.py:355
  42.7 1.3 copy-done.8
  44.5 15.8 %forward.3 = (bf16[1024,768]{1,0:T(8,128)(2,1)S(1)}, f32[8,1024]{1,0:T(8,128)S(1)}, f32[1024,384]{1,0:T(8,128)S(1)}, f32[1024,384]{1,0:T(8,128)}, f32[1024,384]{...) custom-call(bf16[1024,768]{1,0:T(8,128)(2,1)} %get-tuple-element.175, ...), custom_call_target="tpu_custom_call" | custom-call | tf_op jit(solution)/shard_map/forward/pallas_call | solution.py:339
  60.3 0.9 copy-done.19
  62.6 0.9 constant_dynamic-slice_fusion.3
  63.6 1.6 copy-done.37
  66.9 1.2 constant_dynamic-update-slice_fusion.4
  68.8 1.5 collective-permute-start.1
  70.3 1.2 constant_dynamic-update-slice_fusion.3
  73.8 1.0 copy-done.28
  74.9 0.9 copy-done.32
  75.7 19.9 %backward.2 = (bf16[1024,1024]{1,0:T(8,128)(2,1)}, f32[8,1024]{1,0:T(8,128)S(1)}, bf16[1024,768]{1,0:T(8,128)(2,1)S(1)}, bf16[1024,384]{1,0:T(8,128)(2,1)S(1)}, ...) custom-call(s32[1]{0:T(128)} %get-tuple-element.191.len_ref, ...), custom_call_target="tpu_custom_call" | custom-call | tf_op jit(solution)/shard_map/backward/pallas_call | solution.py:393
  96.6 1.1 constant_dynamic-slice_fusion.2
  97.7 1.2 fusion.52
  99.0 2.6 fusion.30.cot_ref
  101.6 3.0 %middle.3 = (f32[1024,384]{1,0:T(8,128)S(1)}, f32[8,1024]{1,0:T(8,128)S(1)}) custom-call(s32[1]{0:T(128)} %get-tuple-element.192.len_ref, bf16[1024,768]{1,0:T(8,128)(2,1)S(1)} %fusion.30.cot_ref, f32[1024,384]{1,0:T(8,128)S(1)} %copy-done.1, f32[8,1024]{1,0:T(8,128)S(1)} %get-tuple-element.73.sq_ref, f32[1,384]{1,0:T(1,128)S(1)} %broadcast_in_dim.28.og_ref, ...), custom_call_target="tpu_custom_call" | custom-call | tf_op jit(solution)/shard_map/middle/pallas_call | solution.py:355
  105.2 2.7 add_convert_fusion.3
  108.0 1.5 collective-permute-start.3
  110.1 2.2 add_convert_fusion.2
  112.3 1.5 collective-permute-start.10
  113.8 15.5 %collective-permute-done.8 = f32[8,1024]{1,0:T(8,128)S(1)} collective-permute-done((f32[8,1024]{1,0:T(8,128)S(1)}, f32[8,1024]{1,0:T(8,128)S(1)}, u32[]{:S(2)}, u32[]{:S(2)}) %collective-permute-start.8) | collective-permute-done | bytes 32800 | tf_op jit(solution)/shard_map/ppermute | solution.py:411
  129.3 19.7 %backward.3 = (bf16[1024,1024]{1,0:T(8,128)(2,1)}, f32[8,1024]{1,0:T(8,128)S(1)}, bf16[1024,768]{1,0:T(8,128)(2,1)S(1)}, bf16[1024,384]{1,0:T(8,128)(2,1)S(1)}, ...) custom-call(s32[1]{0:T(128)} %get-tuple-element.192.len_ref, ...), custom_call_target="tpu_custom_call" | custom-call | tf_op jit(solution)/shard_map/backward/pallas_call | solution.py:393
  149.0 1.1 copy-done.16
  150.1 0.9 copy-done.36
  151.6 2.4 convolution_convert_fusion
  154.1 0.9 fusion.43
  155.1 1.5 collective-permute-start.22
  156.7 1.2 constant_dynamic-slice_fusion.1
  158.0 3.3 %fusion.34 = bf16[768,384]{1,0:T(8,128)(2,1)S(1)} fusion(bf16[1024,384]{1,0:T(8,128)(2,1)} %copy-done.36, bf16[1024,384]{1,0:T(8,128)(2,1)} %copy-done.35, bf16[1024,768]{1,0:T(8,128)(2,1)S(1)} %fusion.30.cot_ref, bf16[1024,768]{1,0:T(8,128)(2,1)S(1)} %copy-done.4), kind=kOutput, calls=%fused_computation.53 | convolution fusion | flops 1217691648 | bytes 5308416 | tf_op jit(solution)/shard_map/dot_general | solution.py:23
  161.4 5.4 %fusion.13 = bf16[768,1024]{1,0:T(8,128)(2,1)S(1)} fusion(bf16[2048,768]{1,0:T(8,128)(2,1)} %constant_dynamic-update-slice_fusion.3, bf16[1024,1024]{1,0:T(8,128)(2,1)S(1)} %copy-done.63, bf16[1024,1024]{1,0:T(8,128)(2,1)S(1)} %copy-done.62), kind=kOutput, calls=%fused_computation.23 | convolution fusion | flops 3230400512 | bytes 8912896 | tf_op jit(solution)/shard_map/dot_general | solution.py:23
  167.0 1.2 dynamic-slice_bitcast_fusion
  169.6 1.3 add_convert_fusion.1
  171.0 1.6 collective-permute-start.23
  172.6 2.2 collective-permute-done.23
  175.8 3.7 %collective-permute-done.24 = f32[4370]{0:T(1024)S(1)} collective-permute-done((f32[4370]{0:T(1024)S(1)}, f32[4370]{0:T(1024)S(1)}, u32[]{:S(2)}, u32[]{:S(2)}) %collective-permute-start.24) | collective-permute-done | bytes 17512 | tf_op jit(solution)/shard_map/ppermute | solution.py:411
  179.5 1.5 collective-permute-start.14
  183.7 13.3 %collective-permute-done.19 = bf16[4,96,1416]{2,1,0:T(8,128)(2,1)} collective-permute-done((bf16[4,96,1416]{2,1,0:T(8,128)(2,1)}, bf16[4,96,1416]{2,1,0:T(8,128)(2,1)}, u32[]{:S(2)}, u32[]{:S(2)}) %collective-permute-start.19) | collective-permute-done | bytes 1087520 | tf_op jit(solution)/shard_map/ppermute | solution.py:411
  196.9 1.9 fusion.8
  198.9 1.6 collective-permute-start.20
  200.5 14.0 %collective-permute-done.17 = bf16[512,768]{1,0:T(8,128)(2,1)} collective-permute-done((bf16[512,768]{1,0:T(8,128)(2,1)S(1)}, bf16[512,768]{1,0:T(8,128)(2,1)}, u32[]{:S(2)}, u32[]{:S(2)}) %collective-permute-start.17) | collective-permute-done | bytes 786464 | tf_op jit(solution)/shard_map/ppermute | solution.py:411
  214.5 2.5 fusion.21
  217.6 3.4 %fusion.20 = (bf16[512,768]{1,0:T(8,128)(2,1)}, bf16[512,768]{1,0:T(8,128)(2,1)S(1)}) fusion(bf16[512,768]{1,0:T(8,128)(2,1)} %collective-permute-done.17, bf16[512,768]{1,0:T(8,128)(2,1)S(1)} %add_convert_fusion, f32[512]{0:T(512)S(1)} %broadcast_multiply_fusion, f32[512]{0:T(512)S(1)} %copy-done.51, bf16[1024,768]{1,0:T(8,128)(2,1)S(1)} %fusion.30.cot_ref, ...), kind=kLoop, calls=%fused_computation.28 | loop fusion | flops 7077888 | bytes 6300676 | tf_op jit(solution)/shard_map/convert_element_type | solution.py:527
  221.0 2.6 collective-permute-start.11
  223.6 25.4 %collective-permute-done.21 = bf16[1,96,1416]{2,1,0:T(8,128)(2,1)S(1)} collective-permute-done((bf16[1,96,1416]{2,1,0:T(8,128)(2,1)S(1)}, bf16[1,96,1416]{2,1,0:T(8,128)(2,1)S(1)}, u32[]{:S(2)}, u32[]{:S(2)}) %collective-permute-start.21) | collective-permute-done | bytes 271904 | tf_op jit(solution)/shard_map/ppermute | solution.py:411
  249.4 2.6 fusion.25
  252.6 1.6 collective-permute-start.26
  254.2 10.6 %collective-permute-done.11 = bf16[512,768]{1,0:T(8,128)(2,1)S(1)} collective-permute-done((bf16[512,768]{1,0:T(8,128)(2,1)S(1)}, bf16[512,768]{1,0:T(8,128)(2,1)S(1)}, u32[]{:S(2)}, u32[]{:S(2)}) %collective-permute-start.11) | collective-permute-done | bytes 786464 | tf_op jit(solution)/shard_map/ppermute | solution.py:411
  268.8 2.1 maximum_select_fusion.4
  271.0 1.9 maximum_select_fusion.3
  272.9 1.9 maximum_select_fusion
  274.8 1.9 pad_maximum_fusion.1
  276.8 2.0 maximum_select_fusion.2
  278.8 1.9 pad_maximum_fusion
  (233 shorter events, 23.0 us)
Async XLA Ops:
  4.5 5.1 %copy-start.64 = (f32[6]{0:T(128)S(1)}, f32[6]{0:T(128)}, u32[]{:S(2)}) copy-start(f32[6]{0:T(128)} %param.34) | copy-start | bytes 76
  4.5 5.1 %copy-start.58 = (f32[384]{0:T(512)S(1)}, f32[384]{0:T(512)}, u32[]{:S(2)}) copy-start(f32[384]{0:T(512)} %param.36) | copy-start | bytes 4612
  4.5 5.1 %copy-start.49 = (f32[768]{0:T(1024)S(1)}, f32[768]{0:T(1024)}, u32[]{:S(2)}) copy-start(f32[768]{0:T(1024)} %param.24) | copy-start | bytes 9220
  4.5 5.1 %copy-start.61 = (f32[6]{0:T(128)S(1)}, f32[6]{0:T(128)}, u32[]{:S(2)}) copy-start(f32[6]{0:T(128)} %param.33) | copy-start | bytes 76
  4.5 5.2 %copy-start.56 = (f32[384]{0:T(512)S(1)}, f32[384]{0:T(512)}, u32[]{:S(2)}) copy-start(f32[384]{0:T(512)} %param.30) | copy-start | bytes 4612
  4.5 5.2 %copy-start.59 = (f32[256]{0:T(256)S(1)}, f32[256]{0:T(256)}, u32[]{:S(2)}) copy-start(f32[256]{0:T(256)} %param.32) | copy-start | bytes 3076
  4.5 5.2 %copy-start.60 = (f32[6]{0:T(128)S(1)}, f32[6]{0:T(128)}, u32[]{:S(2)}) copy-start(f32[6]{0:T(128)} %param.35) | copy-start | bytes 76
  4.5 5.4 %copy-start.46 = (bf16[768,384]{1,0:T(8,128)(2,1)S(1)}, bf16[768,384]{1,0:T(8,128)(2,1)}, u32[]{:S(2)}) copy-start(bf16[768,384]{1,0:T(8,128)(2,1)} %param.25) | copy-start | bytes 1769476
  4.5 6.3 %copy-start.52 = (bf16[768,6]{0,1:T(8,128)(2,1)S(1)}, bf16[768,6]{0,1:T(8,128)(2,1)}, u32[]{:S(2)}) copy-start(bf16[768,6]{0,1:T(8,128)(2,1)} %param.28) | copy-start | bytes 27652
  4.5 6.3 %copy-start.54 = (f32[4,384]{1,0:T(4,128)S(1)}, f32[4,384]{1,0:T(4,128)}, u32[]{:S(2)}) copy-start(f32[4,384]{1,0:T(4,128)} %param.29) | copy-start | bytes 18436
  4.6 6.3 %copy-start.55 = (f32[4,256]{1,0:T(4,128)S(1)}, f32[4,256]{1,0:T(4,128)}, u32[]{:S(2)}) copy-start(f32[4,256]{1,0:T(4,128)} %param.31) | copy-start | bytes 12292
  4.6 6.3 %copy-start.47 = (bf16[768,384]{1,0:T(8,128)(2,1)S(1)}, bf16[768,384]{1,0:T(8,128)(2,1)}, u32[]{:S(2)}) copy-start(bf16[768,384]{1,0:T(8,128)(2,1)} %param.26) | copy-start | bytes 1769476
  5.5 6.3 %copy-start.48 = (bf16[768,256]{1,0:T(8,128)(2,1)S(1)}, bf16[768,256]{1,0:T(8,128)(2,1)}, u32[]{:S(2)}) copy-start(bf16[768,256]{1,0:T(8,128)(2,1)} %param.27) | copy-start | bytes 1179652
  5.5 60.8 %collective-permute-start.5 = (bf16[512,768]{1,0:T(8,128)(2,1)}, bf16[512,768]{1,0:T(8,128)(2,1)}, u32[]{:S(2)}, u32[]{:S(2)}) collective-permute-start(bf16[512,768]{1,0:T(8,128)(2,1)} %dynamic-slice_bitcast_fusion.1), channel_id=1, source_target_pairs={{0,16},{4,20},{8,24},{12,28},{16,0},{20,4},{24,8},{28,12},{1,17},{... | collective-permute-start | bytes 2359304 | tf_op jit(solution)/shard_map/ppermute | solution.py:411
  12.6 4.8 %copy-start = (bf16[384,768]{1,0:T(8,128)(2,1)S(1)}, bf16[384,768]{1,0:T(8,128)(2,1)}, u32[]{:S(2)}) copy-start(bf16[384,768]{1,0:T(8,128)(2,1)} %wout_ref.7) | copy-start | bytes 1769476
  12.6 4.8 %copy-start.5 = (bf16[48,1152]{1,0:T(8,128)(2,1)S(1)}, bf16[48,1152]{1,0:T(8,128)(2,1)}, u32[]{:S(2)}) copy-start(bf16[48,1152]{1,0:T(8,128)(2,1)} %constant.77.clone.spread_ref) | copy-start | bytes 331780
  37.9 67.4 %collective-permute-start.2 = (bf16[512,768]{1,0:T(8,128)(2,1)}, bf16[512,768]{1,0:T(8,128)(2,1)}, u32[]{:S(2)}, u32[]{:S(2)}) collective-permute-start(bf16[512,768]{1,0:T(8,128)(2,1)} %constant_dynamic-slice_fusion.5), channel_id=1, source_target_pairs={{0,1},{1,0},{2,3},{3,2},{4,5},{5,4},{6,7},{7,6},{8,9},{9,8},{10,11... | collective-permute-start | bytes 2359304 | tf_op jit(solution)/shard_map/ppermute | solution.py:411
  44.0 24.2 %collective-permute-start = (f32[8,1024]{1,0:T(8,128)S(1)}, f32[8,1024]{1,0:T(8,128)S(1)}, u32[]{:S(2)}, u32[]{:S(2)}) collective-permute-start(f32[8,1024]{1,0:T(8,128)S(1)} %get-tuple-element.70), channel_id=1, source_target_pairs={{0,1},{1,0},{2,3},{3,2},{4,5},{5,4},{6,7},{7,6},{8,9},{9,8},{10,11... | collective-permute-start | bytes 98312 | tf_op jit(solution)/shard_map/ppermute | solution.py:411
  44.5 21.0 %copy-start.39 = (bf16[1,1024,768]{2,1,0:T(8,128)(2,1)S(1)}, bf16[1,1024,768]{2,1,0:T(8,128)(2,1)}, u32[]{:S(2)}) copy-start(bf16[1,1024,768]{2,1,0:T(8,128)(2,1)} %get-tuple-element.176) | copy-start | bytes 4718596
  62.6 4.3 %copy-start.44 = (bf16[1024,768]{1,0:T(8,128)(2,1)S(1)}, bf16[1024,768]{1,0:T(8,128)(2,1)}, u32[]{:S(2)}) copy-start(bf16[1024,768]{1,0:T(8,128)(2,1)} %get-tuple-element.102) | copy-start | bytes 4718596
  63.6 46.5 %collective-permute-start.9 = (bf16[512,768]{1,0:T(8,128)(2,1)}, bf16[512,768]{1,0:T(8,128)(2,1)}, u32[]{:S(2)}, u32[]{:S(2)}) collective-permute-start(bf16[512,768]{1,0:T(8,128)(2,1)} %constant_dynamic-slice_fusion.3), channel_id=1, source_target_pairs={{0,1},{1,0},{2,3},{3,2},{4,5},{5,4},{6,7},{7,6},{8,9},{9,8},{10,11... | collective-permute-start | bytes 2359304 | tf_op jit(solution)/shard_map/ppermute | solution.py:411
  66.3 32.7 %collective-permute-start.6 = (bf16[512,768]{1,0:T(8,128)(2,1)}, bf16[512,768]{1,0:T(8,128)(2,1)}, u32[]{:S(2)}, u32[]{:S(2)}) collective-permute-start(bf16[512,768]{1,0:T(8,128)(2,1)} %collective-permute-done.5), channel_id=1, source_target_pairs={{0,1},{1,0},{2,3},{3,2},{4,5},{5,4},{6,7},{7,6},{8,9},{9,8},{10,11... | collective-permute-start | bytes 2359304 | tf_op jit(solution)/shard_map/ppermute | solution.py:411
  68.8 4.2 %collective-permute-start.1 = (f32[8,1024]{1,0:T(8,128)}, f32[8,1024]{1,0:T(8,128)}, u32[]{:S(2)}, u32[]{:S(2)}) collective-permute-start(f32[8,1024]{1,0:T(8,128)} %add.204), channel_id=1, source_target_pairs={{0,2},{1,3},{2,0},{3,1},{4,6},{5,7},{6,4},{7,5},{8,10},{9,11},{10,... | collective-permute-start | bytes 98312 | tf_op jit(solution)/shard_map/ppermute | solution.py:411
  70.3 3.5 %copy-start.22 = (bf16[1024,384]{1,0:T(8,128)(2,1)S(1)}, bf16[1024,384]{1,0:T(8,128)(2,1)}, u32[]{:S(2)}) copy-start(bf16[1024,384]{1,0:T(8,128)(2,1)} %copy-done.21) | copy-start | bytes 2359300
  70.3 3.5 %copy-start.24 = (bf16[1024,384]{1,0:T(8,128)(2,1)S(1)}, bf16[1024,384]{1,0:T(8,128)(2,1)}, u32[]{:S(2)}) copy-start(bf16[1024,384]{1,0:T(8,128)(2,1)} %copy-done.23) | copy-start | bytes 2359300
  75.7 23.2 %copy-start.42 = (bf16[2,1024,768]{2,1,0:T(8,128)(2,1)S(1)}, bf16[2,1024,768]{2,1,0:T(8,128)(2,1)}, u32[]{:S(2)}) copy-start(bf16[2,1024,768]{2,1,0:T(8,128)(2,1)} %param.21) | copy-start | bytes 9437188
  96.6 5.0 %copy-start.12 = (bf16[1024,768]{1,0:T(8,128)(2,1)}, bf16[1024,768]{1,0:T(8,128)(2,1)S(1)}, u32[]{:S(2)}) copy-start(bf16[1024,768]{1,0:T(8,128)(2,1)S(1)} %get-tuple-element.88) | copy-start | bytes 4718596
  96.6 5.0 %copy-start.33 = (f32[8,768]{1,0:T(8,128)}, f32[8,768]{1,0:T(8,128)S(1)}, u32[]{:S(2)}) copy-start(f32[8,768]{1,0:T(8,128)S(1)} %get-tuple-element.110) | copy-start | bytes 73732
  97.6 70.6 %collective-permute-start.13 = (bf16[512,768]{1,0:T(8,128)(2,1)}, bf16[512,768]{1,0:T(8,128)(2,1)}, u32[]{:S(2)}, u32[]{:S(2)}) collective-permute-start(bf16[512,768]{1,0:T(8,128)(2,1)} %constant_dynamic-slice_fusion.2), channel_id=1, source_target_pairs={{0,1},{1,0},{2,3},{3,2},{4,5},{5,4},{6,7},{7,6},{8,9},{9,8},{10,11... | collective-permute-start | bytes 2359304 | tf_op jit(solution)/shard_map/ppermute | solution.py:411
  101.6 3.6 %copy-start.11 = (bf16[1024,768]{1,0:T(8,128)(2,1)S(1)}, bf16[1024,768]{1,0:T(8,128)(2,1)}, u32[]{:S(2)}) copy-start(bf16[1024,768]{1,0:T(8,128)(2,1)} %copy-done.10) | copy-start | bytes 4718596
  104.7 7.6 %copy-start.9 = (f32[1024,384]{1,0:T(8,128)}, f32[1024,384]{1,0:T(8,128)S(1)}, u32[]{:S(2)}) copy-start(f32[1024,384]{1,0:T(8,128)S(1)} %get-tuple-element.89.nog_ref) | copy-start | bytes 4718596
  104.7 5.4 %copy-start.15 = (bf16[1024,768]{1,0:T(8,128)(2,1)S(1)}, bf16[1024,768]{1,0:T(8,128)(2,1)}, u32[]{:S(2)}) copy-start(bf16[1024,768]{1,0:T(8,128)(2,1)} %copy-done.14) | copy-start | bytes 4718596
  104.7 4.8 %collective-permute-start.7 = (f32[8,1024]{1,0:T(8,128)S(1)}, f32[8,1024]{1,0:T(8,128)S(1)}, u32[]{:S(2)}, u32[]{:S(2)}) collective-permute-start(f32[8,1024]{1,0:T(8,128)S(1)} %get-tuple-element.74), channel_id=1, source_target_pairs={{0,1},{1,0},{2,3},{3,2},{4,5},{5,4},{6,7},{7,6},{8,9},{9,8},{10,11... | collective-permute-start | bytes 98312 | tf_op jit(solution)/shard_map/ppermute | solution.py:411
  107.9 21.3 %copy-start.20 = (bf16[1024,384]{1,0:T(8,128)(2,1)S(1)}, bf16[1024,384]{1,0:T(8,128)(2,1)}, u32[]{:S(2)}) copy-start(bf16[1024,384]{1,0:T(8,128)(2,1)} %copy-done.19) | copy-start | bytes 2359300
  107.9 21.3 %copy-start.26 = (bf16[1024,256]{1,0:T(8,128)(2,1)S(1)}, bf16[1024,256]{1,0:T(8,128)(2,1)}, u32[]{:S(2)}) copy-start(bf16[1024,256]{1,0:T(8,128)(2,1)} %copy-done.25) | copy-start | bytes 1572868
  108.0 21.3 %copy-start.30 = (f32[24,1024]{1,0:T(8,128)S(1)}, f32[24,1024]{1,0:T(8,128)}, u32[]{:S(2)}) copy-start(f32[24,1024]{1,0:T(8,128)} %copy-done.29) | copy-start | bytes 294916
  108.0 141.4 %collective-permute-start.3 = (bf16[512,768]{1,0:T(8,128)(2,1)}, bf16[512,768]{1,0:T(8,128)(2,1)}, u32[]{:S(2)}, u32[]{:S(2)}) collective-permute-start(bf16[512,768]{1,0:T(8,128)(2,1)} %add_convert_fusion.3), channel_id=1, source_target_pairs={{0,2},{1,3},{2,0},{3,1},{4,6},{5,7},{6,4},{7,5},{8,10},{9,11},{10,... | collective-permute-start | bytes 2359304 | tf_op jit(solution)/shard_map/ppermute | solution.py:411
  109.5 19.8 %collective-permute-start.8 = (f32[8,1024]{1,0:T(8,128)S(1)}, f32[8,1024]{1,0:T(8,128)S(1)}, u32[]{:S(2)}, u32[]{:S(2)}) collective-permute-start(f32[8,1024]{1,0:T(8,128)S(1)} %add.213), channel_id=1, source_target_pairs={{0,2},{1,3},{2,0},{3,1},{4,6},{5,7},{6,4},{7,5},{8,10},{9,11},{10,... | collective-permute-start | bytes 98312 | tf_op jit(solution)/shard_map/ppermute | solution.py:411
  112.3 105.3 %collective-permute-start.10 = (bf16[512,768]{1,0:T(8,128)(2,1)}, bf16[512,768]{1,0:T(8,128)(2,1)}, u32[]{:S(2)}, u32[]{:S(2)}) collective-permute-start(bf16[512,768]{1,0:T(8,128)(2,1)} %add_convert_fusion.2), channel_id=1, source_target_pairs={{0,2},{1,3},{2,0},{3,1},{4,6},{5,7},{6,4},{7,5},{8,10},{9,11},{10,... | collective-permute-start | bytes 2359304 | tf_op jit(solution)/shard_map/ppermute | solution.py:411
  154.0 4.0 %copy-start.4 = (bf16[1024,768]{1,0:T(8,128)(2,1)S(1)}, bf16[1024,768]{1,0:T(8,128)(2,1)}, u32[]{:S(2)}) copy-start(bf16[1024,768]{1,0:T(8,128)(2,1)} %get-tuple-element.171.cot_ref) | copy-start | bytes 4718596
  155.1 15.9 %collective-permute-start.22 = (f32[4370]{0:T(1024)S(1)}, f32[4370]{0:T(1024)S(1)}, u32[]{:S(2)}, u32[]{:S(2)}) collective-permute-start(f32[4370]{0:T(1024)S(1)} %concatenate.174), channel_id=1, source_target_pairs={{0,4},{4,0},{8,12},{12,8},{16,20},{20,16},{24,28},{28,24},{1,5},{5... | collective-permute-start | bytes 52448 | tf_op jit(solution)/shard_map/ppermute | solution.py:411
  157.9 23.7 %collective-permute-start.16 = (bf16[512,768]{1,0:T(8,128)(2,1)S(1)}, bf16[512,768]{1,0:T(8,128)(2,1)S(1)}, u32[]{:S(2)}, u32[]{:S(2)}) collective-permute-start(bf16[512,768]{1,0:T(8,128)(2,1)S(1)} %constant_dynamic-slice_fusion.1), channel_id=1, source_target_pairs={{0,1},{1,0},{2,3},{3,2},{4,5},{5,4},{6,7},{7,6},{8,9},{9,8},{10,11... | collective-permute-start | bytes 2359304 | tf_op jit(solution)/shard_map/ppermute | solution.py:411
  167.0 14.8 %copy-start.41 = (bf16[4,2,96,1416]{3,2,0,1:T(8,128)(2,1)}, bf16[4,2,96,1416]{3,2,0,1:T(8,128)(2,1)S(1)}, u32[]{:S(2)}) copy-start(bf16[4,2,96,1416]{3,2,0,1:T(8,128)(2,1)S(1)} %pad_maximum_fusion.2) | copy-start | bytes 6524932
  168.3 13.4 %copy-start.17 = (bf16[1024,768]{1,0:T(8,128)(2,1)S(1)}, bf16[1024,768]{1,0:T(8,128)(2,1)}, u32[]{:S(2)}) copy-start(bf16[1024,768]{1,0:T(8,128)(2,1)} %copy-done.16) | copy-start | bytes 4718596
  168.3 28.7 %collective-permute-start.19 = (bf16[4,96,1416]{2,1,0:T(8,128)(2,1)}, bf16[4,96,1416]{2,1,0:T(8,128)(2,1)}, u32[]{:S(2)}, u32[]{:S(2)}) collective-permute-start(bf16[4,96,1416]{2,1,0:T(8,128)(2,1)} %dynamic-slice_bitcast_fusion), channel_id=1, source_target_pairs={{0,4},{4,0},{8,12},{12,8},{16,20},{20,16},{24,28},{28,24},{1,5},{5... | collective-permute-start | bytes 3262472 | tf_op jit(solution)/shard_map/ppermute | solution.py:411
  171.0 3.8 %collective-permute-start.23 = (f32[4370]{0:T(1024)S(1)}, f32[4370]{0:T(1024)S(1)}, u32[]{:S(2)}, u32[]{:S(2)}) collective-permute-start(f32[4370]{0:T(1024)S(1)} %add.241), channel_id=1, source_target_pairs={{0,8},{4,12},{8,0},{12,4},{16,24},{20,28},{24,16},{28,20},{1,9},{5... | collective-permute-start | bytes 52448 | tf_op jit(solution)/shard_map/ppermute | solution.py:411
  174.8 4.7 %collective-permute-start.24 = (f32[4370]{0:T(1024)S(1)}, f32[4370]{0:T(1024)S(1)}, u32[]{:S(2)}, u32[]{:S(2)}) collective-permute-start(f32[4370]{0:T(1024)S(1)} %add.242), channel_id=1, source_target_pairs={{0,16},{4,20},{8,24},{12,28},{16,0},{20,4},{24,8},{28,12},{1,17},{... | collective-permute-start | bytes 52448 | tf_op jit(solution)/shard_map/ppermute | solution.py:411
  179.5 21.0 %collective-permute-start.14 = (bf16[512,768]{1,0:T(8,128)(2,1)S(1)}, bf16[512,768]{1,0:T(8,128)(2,1)}, u32[]{:S(2)}, u32[]{:S(2)}) collective-permute-start(bf16[512,768]{1,0:T(8,128)(2,1)S(1)} %add_convert_fusion.1), channel_id=1, source_target_pairs={{0,2},{1,3},{2,0},{3,1},{4,6},{5,7},{6,4},{7,5},{8,10},{9,11},{10,... | collective-permute-start | bytes 2359304 | tf_op jit(solution)/shard_map/ppermute | solution.py:411
  181.9 32.6 %collective-permute-start.17 = (bf16[512,768]{1,0:T(8,128)(2,1)S(1)}, bf16[512,768]{1,0:T(8,128)(2,1)}, u32[]{:S(2)}, u32[]{:S(2)}) collective-permute-start(bf16[512,768]{1,0:T(8,128)(2,1)S(1)} %add_convert_fusion), channel_id=1, source_target_pairs={{0,2},{1,3},{2,0},{3,1},{4,6},{5,7},{6,4},{7,5},{8,10},{9,11},{10,... | collective-permute-start | bytes 2359304 | tf_op jit(solution)/shard_map/ppermute | solution.py:411
  183.7 30.9 %copy-start.38 = (bf16[1,1024,768]{2,1,0:T(8,128)(2,1)S(1)}, bf16[1,1024,768]{2,1,0:T(8,128)(2,1)}, u32[]{:S(2)}) copy-start(bf16[1,1024,768]{2,1,0:T(8,128)(2,1)} %get-tuple-element.173) | copy-start | bytes 4718596
  183.7 30.9 %copy-start.40 = (bf16[1,1024,768]{2,1,0:T(8,128)(2,1)S(1)}, bf16[1,1024,768]{2,1,0:T(8,128)(2,1)}, u32[]{:S(2)}) copy-start(bf16[1,1024,768]{2,1,0:T(8,128)(2,1)} %get-tuple-element.176) | copy-start | bytes 4718596
  183.7 30.9 %copy-start.50 = (f32[512]{0:T(512)S(1)}, f32[512]{0:T(512)}, u32[]{:S(2)}) copy-start(f32[512]{0:T(512)} %add_rsqrt_fusion.1) | copy-start | bytes 6148
  183.7 30.9 %copy-start.51 = (f32[512]{0:T(512)S(1)}, f32[512]{0:T(512)}, u32[]{:S(2)}) copy-start(f32[512]{0:T(512)} %add_rsqrt_fusion) | copy-start | bytes 6148
  198.9 18.1 %collective-permute-start.20 = (bf16[2,96,1416]{2,1,0:T(8,128)(2,1)S(1)}, bf16[2,96,1416]{2,1,0:T(8,128)(2,1)S(1)}, u32[]{:S(2)}, u32[]{:S(2)}) collective-permute-start(bf16[2,96,1416]{2,1,0:T(8,128)(2,1)S(1)} %dynamic-slice_bitcast_fusion.2), channel_id=1, source_target_pairs={{0,8},{4,12},{8,0},{12,4},{16,24},{20,28},{24,16},{28,20},{1,9},{5... | collective-permute-start | bytes 1631240 | tf_op jit(solution)/shard_map/ppermute | solution.py:411
  217.2 31.9 %collective-permute-start.21 = (bf16[1,96,1416]{2,1,0:T(8,128)(2,1)S(1)}, bf16[1,96,1416]{2,1,0:T(8,128)(2,1)S(1)}, u32[]{:S(2)}, u32[]{:S(2)}) collective-permute-start(bf16[1,96,1416]{2,1,0:T(8,128)(2,1)S(1)} %constant_dynamic-slice_fusion), channel_id=1, source_target_pairs={{0,16},{4,20},{8,24},{12,28},{16,0},{20,4},{24,8},{28,12},{1,17},{... | collective-permute-start | bytes 815624 | tf_op jit(solution)/shard_map/ppermute | solution.py:411
  221.0 28.4 %copy-start.43 = (bf16[1,1024,768]{2,1,0:T(8,128)(2,1)S(1)}, bf16[1,1024,768]{2,1,0:T(8,128)(2,1)}, u32[]{:S(2)}) copy-start(bf16[1,1024,768]{2,1,0:T(8,128)(2,1)} %get-tuple-element.170) | copy-start | bytes 4718596
  221.0 28.4 %copy-start.53 = (f32[512]{0:T(512)S(1)}, f32[512]{0:T(512)}, u32[]{:S(2)}) copy-start(f32[512]{0:T(512)} %fusion.52) | copy-start | bytes 6148
  221.0 47.8 %collective-permute-start.18 = (bf16[512,768]{1,0:T(8,128)(2,1)}, bf16[512,768]{1,0:T(8,128)(2,1)S(1)}, u32[]{:S(2)}, u32[]{:S(2)}) collective-permute-start(bf16[512,768]{1,0:T(8,128)(2,1)} %get-tuple-element.179), channel_id=1, source_target_pairs={{0,1},{1,0},{2,3},{3,2},{4,5},{5,4},{6,7},{7,6},{8,9},{9,8},{10,11... | collective-permute-start | bytes 2359304 | tf_op jit(solution)/shard_map/ppermute | solution.py:411
  221.0 43.8 %collective-permute-start.11 = (bf16[512,768]{1,0:T(8,128)(2,1)S(1)}, bf16[512,768]{1,0:T(8,128)(2,1)S(1)}, u32[]{:S(2)}, u32[]{:S(2)}) collective-permute-start(bf16[512,768]{1,0:T(8,128)(2,1)S(1)} %get-tuple-element.180), channel_id=1, source_target_pairs={{0,16},{4,20},{8,24},{12,28},{16,0},{20,4},{24,8},{28,12},{1,17},{... | collective-permute-start | bytes 2359304 | tf_op jit(solution)/shard_map/ppermute | solution.py:411
  249.2 3.3 %collective-permute-start.25 = (f32[26624]{0:T(1024)S(1)}, f32[26624]{0:T(1024)S(1)}, u32[]{:S(2)}, u32[]{:S(2)}) collective-permute-start(f32[26624]{0:T(1024)S(1)} %pad_maximum_fusion.3), channel_id=1, source_target_pairs={{0,1},{1,0},{2,3},{3,2},{4,5},{5,4},{6,7},{7,6},{8,9},{9,8},{10,11... | collective-permute-start | bytes 319496 | tf_op jit(solution)/shard_map/ppermute | solution.py:411
  251.9 19.0 %collective-permute-start.15 = (bf16[512,768]{1,0:T(8,128)(2,1)S(1)}, bf16[512,768]{1,0:T(8,128)(2,1)}, u32[]{:S(2)}, u32[]{:S(2)}) collective-permute-start(bf16[512,768]{1,0:T(8,128)(2,1)S(1)} %get-tuple-element.177), channel_id=1, source_target_pairs={{0,1},{1,0},{2,3},{3,2},{4,5},{5,4},{6,7},{7,6},{8,9},{9,8},{10,11... | collective-permute-start | bytes 2359304 | tf_op jit(solution)/shard_map/ppermute | solution.py:411
  252.5 20.4 %collective-permute-start.4 = (bf16[512,768]{1,0:T(8,128)(2,1)S(1)}, bf16[512,768]{1,0:T(8,128)(2,1)}, u32[]{:S(2)}, u32[]{:S(2)}) collective-permute-start(bf16[512,768]{1,0:T(8,128)(2,1)S(1)} %get-tuple-element.178), channel_id=1, source_target_pairs={{0,1},{1,0},{2,3},{3,2},{4,5},{5,4},{6,7},{7,6},{8,9},{9,8},{10,11... | collective-permute-start | bytes 2359304 | tf_op jit(solution)/shard_map/ppermute | solution.py:411
  252.6 13.8 %collective-permute-start.26 = (f32[26624]{0:T(1024)S(1)}, f32[26624]{0:T(1024)S(1)}, u32[]{:S(2)}, u32[]{:S(2)}) collective-permute-start(f32[26624]{0:T(1024)S(1)} %fusion.59), channel_id=1, source_target_pairs={{0,2},{1,3},{2,0},{3,1},{4,6},{5,7},{6,4},{7,5},{8,10},{9,11},{10,... | collective-permute-start | bytes 319496 | tf_op jit(solution)/shard_map/ppermute | solution.py:411
  264.8 11.9 %collective-permute-start.12 = (bf16[512,768]{1,0:T(8,128)(2,1)S(1)}, bf16[512,768]{1,0:T(8,128)(2,1)}, u32[]{:S(2)}, u32[]{:S(2)}) collective-permute-start(bf16[512,768]{1,0:T(8,128)(2,1)S(1)} %broadcast_select_fusion), channel_id=1, source_target_pairs={{0,1},{1,0},{2,3},{3,2},{4,5},{5,4},{6,7},{7,6},{8,9},{9,8},{10,11... | collective-permute-start | bytes 2359304 | tf_op jit(solution)/shard_map/ppermute | solution.py:411
  (29 other events, 52.5 us)
